TPU v7x, 512 devices: a whole 4x4x16 slice. The times are simulated.
512 devices in a mesh: lon: 32 (over z, x_hi), lat: 16 (over y, x_lo, core).
Axes of the slice: x: 4 (x_hi: 2, x_lo: 2; x = x_hi * 2 + x_lo), y: 4, z: 16, core: 2. Of those that a mesh axis runs over, the one named last changes fastest.
Arguments:
- features: bfloat16 [256, 512, 180], P('lat', 'lon'), may hold values from -6 to 6
- cotangent: bfloat16 [256, 512, 180], P('lat', 'lon'), may hold values from -6 to 6
- first_gain: float32 [180], replicated, may hold values from 0.25 to 1.75
- window_qkv: bfloat16 [180, 540], replicated, may hold values from -0.4375 to 0.4375
- window_proj: bfloat16 [180, 180], replicated, may hold values from -0.4375 to 0.4375
- window_table: float32 [6, 961], replicated, may hold values from -3 to 300
- second_gain: float32 [180], replicated, may hold values from 0.25 to 1.75
- cross_qkv: bfloat16 [180, 540], replicated, may hold values from -0.4375 to 0.4375
- cross_proj: bfloat16 [180, 180], replicated, may hold values from -0.4375 to 0.4375
- cross_table: float32 [6, 1521], replicated, may hold values from -3 to 300
Outputs:
- grad_features: float32 [256, 512, 180], P('lat', 'lon')
- grad_window_table: float32 [6, 961], replicated
- grad_cross_table: float32 [6, 1521], replicated
All inputs are finite; a program needn't handle non-finite values.
Results may differ from a plain program's by a relative error of at most 0.017.
Values may be sent and summed in bfloat16 or wider, within the bound.
A program may use at most 192 MiB of HBM per device.

v0:
```python
import functools

import jax
import jax.numpy as jnp
from jax import lax
from jax.experimental import pallas as pl
from jax.experimental.pallas import tpu as pltpu
from jax.sharding import PartitionSpec as P

CHANNELS = 180
HEADS = 6
HEAD_SIZE = 30
HEAD_PAD = 32
WIDE = 256
CELLS = 256
KEYS = 576
KEY_SIDE = 24
SPAN = 31
CROSS = 39
EPSILON = 1e-05
NEGATIVE = -1e30
LOG2E = 1.4426950408889634
SCALE = HEAD_SIZE**-0.5
TILES_W = 8
TILES_C = 12
LANES_W = 1024
LANES_C = 1280
USED_W = 640
USED_C = 896
MESH = pl.DeviceIdType.MESH
F32 = jnp.float32
BF16 = jnp.bfloat16


def iota(shape, dim):
    return lax.broadcasted_iota(jnp.int32, shape, dim)


def dot(a, b):
    return jnp.dot(a, b, preferred_element_type=F32)


def dot_nt(a, b):
    return lax.dot_general(a, b, (((1,), (1,)), ((), ())), preferred_element_type=F32)


def one_hot(mask):
    return jnp.where(mask, 1.0, 0.0).astype(BF16)


def roll(x, shift):
    size = x.shape[-1]
    return pltpu.roll(x, shift % size, x.ndim - 1)


def norm_parts(values):
    centre = jnp.mean(values, axis=-1, keepdims=True)
    offset = values - centre
    spread = jnp.mean(offset * offset, axis=-1, keepdims=True)
    inverse = lax.rsqrt(spread + EPSILON)
    return offset * inverse, inverse


def norm_back(unit, inverse, gain, grads):
    scaled = grads * gain
    first = jnp.mean(scaled, axis=-1, keepdims=True)
    second = jnp.mean(scaled * unit, axis=-1, keepdims=True)
    return inverse * (scaled - first - unit * second)


def slot(a, b):
    return (a // 2 * 2 + b // 2) * 4 + a % 2 * 2 + b % 2


OWN = [(sy, sx, 2 * sy + sx, (1 - sy) * 2 + (1 - sx)) for sy in (0, 1) for sx in (0, 1)]


def spread_rows(base, stride, ways):
    rows = iota(base.shape, 0)
    for bit in (1, 2, 4):
        base = jnp.where((rows & bit) != 0, roll(base, stride * bit), base)
    upper = (iota(base.shape, 1) & 16) != 0
    base = jnp.where(upper, roll(base, -240), base)
    return [base if r == 0 else roll(base, -32 * r) for r in range(ways)]


def gather_rows(parts, stride):
    total = parts[0]
    for r in range(1, len(parts)):
        total = total + roll(parts[r], 32 * r)
    upper = (iota(total.shape, 1) & 16) != 0
    total = jnp.where(upper, 0.0, total) + roll(jnp.where(upper, total, 0.0), 240)
    rows = iota(total.shape, 0)
    for bit in (1, 2, 4):
        total = jnp.where((rows & bit) != 0, roll(total, -stride * bit), total)
    return jnp.sum(total.reshape(HEADS, 8, total.shape[1]), axis=1)


def kernel(
    n_lat,
    n_lon,
    feat_in,
    cot_in_hbm,
    gain1_in,
    qkv1_in,
    proj1_in,
    tab1_in,
    gain2_in,
    qkv2_in,
    proj2_in,
    tab2_in,
    out_ref,
    out1_ref,
    out2_ref,
    feat_ref,
    cot_ref,
    gain1_ref,
    qkv1_ref,
    proj1_ref,
    tab1_ref,
    gain2_ref,
    qkv2_ref,
    proj2_ref,
    tab2_ref,
    load_sem,
    region,
    flat1,
    flat2,
    wt1,
    wt2,
    pp1,
    pp2,
    turn,
    z1,
    z2,
    acc1,
    acc2,
    feats,
    middles,
    units,
    inverses,
    kk,
    vt,
    vv,
    kt,
    qm,
    dom,
    qmt,
    dmt,
    ot,
    p1,
    p2,
    ds1,
    ds2,
    k2,
    v2,
    k2t,
    lin,
    mid_out,
    mid_in,
    back_out,
    back_in,
    dense1,
    dense2,
    tiles1,
    tiles2,
    rs1,
    rs2,
    ag1,
    ag2,
    fin1,
    fin2,
    halo_send,
    halo_recv,
    mid_send,
    mid_recv,
    back_send,
    back_recv,
    sum_send,
    sum_recv,
):
    lat = lax.axis_index("lat")
    lon = lax.axis_index("lon")

    def wrapped(value, count):
        value = jnp.where(value >= count, value - count, value)
        return jnp.where(value < 0, value + count, value)

    def at(dy, dx):
        return (wrapped(lon + dx, n_lon), wrapped(lat + dy, n_lat))

    loads = [
        pltpu.make_async_copy(src, dst, load_sem.at[i])
        for i, (src, dst) in enumerate(
            (
                (feat_in, feat_ref),
                (qkv1_in, qkv1_ref),
                (proj1_in, proj1_ref),
                (gain1_in, gain1_ref),
                (tab1_in, tab1_ref),
                (tab2_in, tab2_ref),
                (qkv2_in, qkv2_ref),
                (gain2_in, gain2_ref),
                (proj2_in, proj2_ref),
                (cot_in_hbm, cot_ref),
            )
        )
    ]
    for load in loads:
        load.start()

    barrier = pltpu.get_barrier_semaphore()

    def greet(dy, dx):
        pl.semaphore_signal(barrier, inc=1, device_id=at(dy, dx), device_id_type=MESH)

    for dy in (-1, 1):
        for dx in (-1, 1):
            greet(dy, dx)
    for j in range(1, n_lat):
        greet(j, 0)
    for j in range(1, n_lon):
        greet(0, j)

    loads[0].wait()
    own = feat_ref[...].astype(F32)
    for sy, sx, w, s in OWN:
        quarter = own[8 * sy : 8 * sy + 8, 8 * sx : 8 * sx + 8, :].reshape(64, CHANNELS)
        region[w * 4 + s] = quarter.astype(BF16)

    for load in loads[1:5]:
        load.wait()

    row = iota((3 * WIDE, 1), 0)
    lane = row & 255
    real = (lane < 192) & ((lane & 31) < HEAD_SIZE)
    source = jnp.where(real, CHANNELS * (row >> 8) + lane - 2 * (lane >> 5), -1)
    pick = one_hot(iota((3 * WIDE, 3 * CHANNELS), 1) == source)
    wt1[...] = dot_nt(pick, qkv1_ref[...]).astype(BF16)
    pick_proj = pick[:WIDE, :CHANNELS]
    pp1[...] = dot(pick_proj, proj1_ref[...]).astype(BF16)

    pl.semaphore_wait(barrier, n_lat - 1 + n_lon - 1 + 4)

    halo = []
    for a in (1, 2):
        for b in (1, 2):
            for dy in (0, -1 if a == 1 else 1):
                for dx in (0, -1 if b == 1 else 1):
                    if dy == 0 and dx == 0:
                        continue
                    halo.append(
                        pltpu.make_async_remote_copy(
                            src_ref=region.at[slot(a, b)],
                            dst_ref=region.at[slot(a - 2 * dy, b - 2 * dx)],
                            send_sem=halo_send,
                            recv_sem=halo_recv,
                            device_id=at(dy, dx),
                            device_id_type=MESH,
                        )
                    )
    for copy in halo:
        copy.start()

    for load in loads[5:]:
        load.wait()
    wt2[...] = dot_nt(pick, qkv2_ref[...]).astype(BF16)
    pp2[...] = dot(pick_proj, proj2_ref[...]).astype(BF16)

    def turned(c):
        r = 255 - c
        return ((r >> 3) & 7) * 32 + ((r >> 7) & 1) * 16 + ((r >> 6) & 1) * 8 + (r & 7)

    turn[0] = one_hot(iota((CELLS, CELLS), 0) == turned(iota((1, CELLS), 1)))
    turn[1] = one_hot(iota((CELLS, CELLS), 1) == turned(iota((CELLS, 1), 0)))

    flat1[...] = jnp.zeros(flat1.shape, F32)
    flat2[...] = jnp.zeros(flat2.shape, F32)
    for dy in range(SPAN):
        flat1[:, dy * 32 : dy * 32 + SPAN] = tab1_ref[:, dy * SPAN : (dy + 1) * SPAN]
    for dy in range(CROSS):
        for s in range(3):
            start = dy * CROSS + 8 * s
            flat2[s, :, dy * 32 : dy * 32 + 23] = tab2_ref[:, start : start + 23]
    for s in range(2):
        base = jnp.broadcast_to(flat1[...][:, None, :] * LOG2E, (HEADS, 8, LANES_W))
        base = roll(base.reshape(HEADS * 8, LANES_W), 8 * s - 15)
        for r, part in enumerate(spread_rows(base, 1, 4)):
            z1[s, r] = part[:, :USED_W].reshape(HEADS, 8, USED_W)
    for s in range(3):
        base = jnp.broadcast_to(flat2[s][:, None, :] * LOG2E, (HEADS, 8, LANES_C))
        base = base.reshape(HEADS * 8, LANES_C)
        for r, part in enumerate(spread_rows(base, -1, 4)):
            z2[s, r] = part[:, :USED_C].reshape(HEADS, 8, USED_C)
    query_half = (iota((1, CELLS), 1) >> 4) & 1

    def window_bias(h, masks):
        pieces = []
        for y8 in range(8):
            for sy in range(2):
                t, r = divmod(15 - (8 * sy + y8), 4)
                for sx in range(2):
                    pieces.append(z1[sx, r, h, :, 128 * t : 128 * t + CELLS] + masks[sy])
        return jnp.concatenate(pieces, axis=0)

    def cross_bias(h):
        pieces = []
        for ky in range(KEY_SIDE):
            t, r = divmod(ky, 4)
            for s in range(3):
                pieces.append(z2[s, r, h, :, 128 * t : 128 * t + CELLS])
        return jnp.concatenate(pieces, axis=0)

    def collect(acc, h, s, count, group_of, slopes):
        for r in range(4):
            for t in range(count // 4 + 1):
                parts = []
                if t < count // 4:
                    group = group_of(4 * t + r)
                    parts.append(slopes[group : group + 8, 0:128])
                if t > 0:
                    group = group_of(4 * t - 4 + r)
                    parts.append(slopes[group : group + 8, 128:256])
                acc[s, r, h, :, 128 * t : 128 * t + 128] = sum(parts[1:], parts[0])

    def head_rows(values, h):
        before, rows = h % 4 * HEAD_PAD, values[h * HEAD_PAD : (h + 1) * HEAD_PAD, :]
        pieces = [rows]
        if before:
            pieces = [jnp.zeros((before, CELLS), values.dtype)] + pieces
        if before + HEAD_PAD < 128:
            pieces.append(jnp.zeros((128 - HEAD_PAD - before, CELLS), values.dtype))
        return jnp.concatenate(pieces, axis=0) if len(pieces) > 1 else rows

    every = region.at[pl.ds(0, 12)]
    pltpu.make_async_copy(every, every, halo_recv).wait()

    gain1 = gain1_ref[...]
    gain2 = gain2_ref[...]
    wide_lane = iota((CELLS, WIDE), 1) >> 5

    def window(w, _):
        parts = [
            region[w * 4 + s].astype(F32).reshape(8, 1, 8, CHANNELS) for s in range(4)
        ]
        values = jnp.concatenate(parts, axis=1).reshape(CELLS, CHANNELS)
        unit, _ = norm_parts(values)
        normed = (unit * gain1).astype(BF16)
        feats[...] = values
        queries = dot_nt(wt1[0:WIDE, :], normed).astype(BF16)
        kk[...] = dot_nt(normed, wt1[WIDE : 2 * WIDE, :]).astype(BF16)
        vt[...] = dot_nt(wt1[2 * WIDE :, :], normed).astype(BF16)
        edge = lat == jnp.where(w < 2, 0, n_lat - 1)
        floor = jnp.where(edge, NEGATIVE, 0.0)
        masks = [jnp.where(query_half != sy, floor, 0.0) for sy in range(2)]
        for h in range(HEADS):
            half = h // 4 * 128
            products = dot(kk[:, half : half + 128], head_rows(queries, h))
            scores = products * (SCALE * LOG2E) + window_bias(h, masks)
            peak = jnp.max(scores, axis=0, keepdims=True)
            raised = jnp.exp2(scores - peak)
            inverse = 1.0 / jnp.sum(raised, axis=0, keepdims=True)
            probs = (raised * inverse).astype(BF16)
            p1[:, h * CELLS : (h + 1) * CELLS] = probs
            ot[h * HEAD_PAD : (h + 1) * HEAD_PAD, :] = dot(
                vt[h * HEAD_PAD : (h + 1) * HEAD_PAD, :], probs
            )
        heads_out = jnp.transpose(ot[...]).astype(BF16)
        middle = values + dot(heads_out, pp1[...])
        middles[w] = middle.reshape(8, 2, 2, 8, CHANNELS)
        return 0

    ot[...] = jnp.zeros(ot.shape, F32)
    lax.fori_loop(0, 4, window, 0)

    y_runs = ((0, 0, 4, 8, 0), (0, 1, 0, 8, 4), (1, 0, 0, 8, 12), (1, 1, 0, 4, 20))
    for wy, sy, first, last, place in y_runs:
        for wx in range(2):
            for sx in range(2):
                start = (2 * wx + sx) * 8
                lin[place : place + last - first, start : start + 8, :] = middles[
                    2 * wy + wx, first:last, sy, sx
                ]
    unit2, inverse2 = norm_parts(lin[...].reshape(KEY_SIDE * 32, CHANNELS))
    units[...] = unit2
    inverses[...] = inverse2
    lin[...] = (unit2 * gain2).astype(BF16).astype(F32).reshape(KEY_SIDE, 32, CHANNELS)
    inside_low = jnp.where(lat > 0, 1.0, 0.0)
    inside_high = jnp.where(lat < n_lat - 1, 1.0, 0.0)
    lin[0:4] = lin[0:4] * inside_low
    lin[20:24] = lin[20:24] * inside_high
    keys_in = lin[:, 4:28, :].reshape(KEYS, CHANNELS).astype(BF16)
    k2[...] = dot_nt(keys_in, wt2[WIDE : 2 * WIDE, :]).astype(BF16)
    v2[...] = dot_nt(keys_in, wt2[2 * WIDE :, :]).astype(BF16)
    k2t[...] = dot_nt(wt2[WIDE : 2 * WIDE, :], keys_in).astype(BF16)

    def own_part(sy, sx):
        return slice(4 + 8 * sy, 12 + 8 * sy), slice(8 + 8 * sx, 16 + 8 * sx)

    own_second = jnp.concatenate(
        [lin[(*own_part(sy, sx), slice(None))].reshape(64, CHANNELS) for sy, sx, w, s in OWN],
        axis=0,
    )
    queries_in = dot(turn[0], own_second.astype(BF16)).astype(BF16)
    cot = cot_ref[...].astype(F32)
    cot_own = [
        cot[8 * sy : 8 * sy + 8, 8 * sx : 8 * sx + 8, :].reshape(64, CHANNELS)
        for sy, sx, w, s in OWN
    ]
    cot_in = dot(turn[0], jnp.concatenate(cot_own, axis=0).astype(BF16)).astype(BF16)
    queries_t = dot_nt(wt2[0:WIDE, :], queries_in).astype(BF16)
    grads_t = dot_nt(pp2[...], cot_in).astype(BF16)
    queries = dot_nt(queries_in, wt2[0:WIDE, :])
    grads = dot_nt(cot_in, pp2[...])
    for h in range(HEADS):
        qmt[h] = head_rows(queries_t, h)
        dmt[h] = head_rows(grads_t, h)
        qm[h * CELLS : (h + 1) * CELLS, :] = jnp.where(wide_lane == h, queries, 0.0).astype(BF16)
        dom[h * CELLS : (h + 1) * CELLS, :] = jnp.where(wide_lane == h, grads, 0.0).astype(BF16)

    def cross_pair(pair, _):
        half = pl.ds(pl.multiple_of(pair // 2 * 128, 128), 128)
        for i in range(2):
            h = 2 * pair + i
            scores = dot(k2[:, half], qmt[h]) * (SCALE * LOG2E) + cross_bias(h)
            peak = jnp.max(scores, axis=0, keepdims=True)
            raised = jnp.exp2(scores - peak)
            inverse = 1.0 / jnp.sum(raised, axis=0, keepdims=True)
            probs = raised * inverse
            columns = pl.ds(pl.multiple_of(h * CELLS, CELLS), CELLS)
            p2[:, columns] = probs.astype(BF16)
            weighted = probs * dot(v2[:, half], dmt[h])
            total = jnp.sum(weighted, axis=0, keepdims=True)
            slopes = weighted - probs * total
            for s in range(3):
                collect(acc2, h, s, KEY_SIDE, lambda m: (m * 3 + s) * 8, slopes)
            slopes_b = slopes.astype(BF16)
            ds2[:, columns] = slopes_b
            rows = pl.ds(pl.multiple_of(h * HEAD_PAD, HEAD_PAD), HEAD_PAD)
            ot[rows, :] = dot(k2t[rows, :], slopes_b)
        return 0

    lax.fori_loop(0, HEADS // 2, cross_pair, 0)
    grad_queries = (jnp.transpose(ot[...]) * SCALE).astype(BF16)
    grad_keys = (dot(ds2[...], qm[...]) * SCALE).astype(BF16)
    grad_values = dot(p2[...], dom[...]).astype(BF16)
    grad_second = dot(grad_keys, wt2[WIDE : 2 * WIDE, :]) + dot(grad_values, wt2[2 * WIDE :, :])
    grad_own = dot(turn[1], dot(grad_queries, wt2[0:WIDE, :]).astype(BF16))

    lin[...] = jnp.zeros(lin.shape, F32)
    lin[:, 4:28, :] = grad_second.reshape(KEY_SIDE, KEY_SIDE, CHANNELS)
    lin[0:4] = lin[0:4] * inside_low
    lin[20:24] = lin[20:24] * inside_high
    for i, (sy, sx, w, s) in enumerate(OWN):
        place = (*own_part(sy, sx), slice(None))
        lin[place] = lin[place] + grad_own[64 * i : 64 * i + 64, :].reshape(8, 8, CHANNELS)
    grad = norm_back(
        units[...], inverses[...], gain2, lin[...].reshape(KEY_SIDE * 32, CHANNELS)
    )
    lin[...] = grad.reshape(KEY_SIDE, 32, CHANNELS)
    for i, (sy, sx, w, s) in enumerate(OWN):
        place = (*own_part(sy, sx), slice(None))
        lin[place] = lin[place] + cot_own[i].reshape(8, 8, CHANNELS)
    for w in range(3):
        rows, cols = 12 * (w // 2), 16 * (w % 2)
        piece = lin[rows : rows + 12, cols : cols + 16, :]
        mid_out[w] = piece.reshape(192, CHANNELS).astype(BF16)
        pltpu.make_async_remote_copy(
            src_ref=mid_out.at[w],
            dst_ref=mid_in.at[w],
            send_sem=mid_send,
            recv_sem=mid_recv,
            device_id=at(w // 2 - 1, w % 2 - 1),
            device_id_type=MESH,
        ).start()

    def sum_scatter(kind, tiles, buffer):
        chunks, depth = buffer_plan(tiles, n_lat)
        for c in range(chunks):

            @pl.when(lat != c)
            def _():
                pltpu.make_async_remote_copy(
                    src_ref=tiles.at[pl.ds(c * depth, depth)],
                    dst_ref=buffer.at[wrapped(lat - c, n_lat) - 1],
                    send_sem=sum_send.at[kind],
                    recv_sem=sum_recv.at[kind],
                    device_id=(lon, c),
                    device_id_type=MESH,
                ).start()

    def drain(sem, ref):
        pltpu.make_async_copy(ref, ref, sem).wait()

    def sum_spread(kind, tiles, buffer, rows):
        chunks, depth = buffer_plan(tiles, n_lat)

        @pl.when(lat < chunks)
        def _():
            drain(sum_recv.at[kind], buffer)
            total = tiles[pl.ds(lat * depth, depth)]
            for i in range(n_lat - 1):
                total = total + buffer[i]
            rows[lon] = total

            for j in range(1, n_lon):
                pltpu.make_async_remote_copy(
                    src_ref=rows.at[lon],
                    dst_ref=rows.at[lon],
                    send_sem=sum_send.at[kind + 1],
                    recv_sem=sum_recv.at[kind + 1],
                    device_id=at(0, j),
                    device_id_type=MESH,
                ).start()

    def sum_gather(kind, tiles, rows, result):
        chunks, depth = buffer_plan(tiles, n_lat)

        @pl.when(lat < chunks)
        def _():
            drain(sum_recv.at[kind + 1], rows.at[pl.ds(0, n_lon - 1)])
            total = rows[0]
            for i in range(1, n_lon):
                total = total + rows[i]
            result[lat] = total

            for j in range(1, n_lat):
                pltpu.make_async_remote_copy(
                    src_ref=result.at[lat],
                    dst_ref=result.at[lat],
                    send_sem=sum_send.at[kind + 2],
                    recv_sem=sum_recv.at[kind + 2],
                    device_id=at(j, 0),
                    device_id_type=MESH,
                ).start()

    def sum_end(kind, tiles, buffer, rows, result):
        chunks, depth = buffer_plan(tiles, n_lat)

        @pl.when(lat < chunks)
        def _():
            if chunks > 1:
                drain(sum_recv.at[kind + 2], result.at[pl.ds(0, chunks - 1)])
                drain(sum_send.at[kind], result.at[pl.ds(0, chunks - 1)])
            drain(sum_send.at[kind + 1], rows.at[pl.ds(0, n_lon - 1)])
            drain(sum_send.at[kind + 2], buffer)

        @pl.when(lat >= chunks)
        def _():
            drain(sum_recv.at[kind + 2], result)
            drain(sum_send.at[kind], result)

    def joined(result, count):
        chunks, depth = result.shape[0], result.shape[1]
        whole = jnp.concatenate(
            [result[c, d] for c in range(chunks) for d in range(depth)], axis=1
        )
        return whole[:HEADS, :count]

    for s in range(3):
        parts = [
            jnp.concatenate(
                [
                    acc2[s, r].reshape(HEADS * 8, USED_C),
                    jnp.zeros((HEADS * 8, LANES_C - USED_C), F32),
                ],
                axis=1,
            )
            for r in range(4)
        ]
        flat2[s] = gather_rows(parts, -1)
    dense2[...] = jnp.zeros(dense2.shape, F32)
    for dy in range(CROSS):
        for s in range(3):
            start = dy * CROSS + 8 * s
            dense2[s, 0:HEADS, start : start + 23] = flat2[s, :, dy * 32 : dy * 32 + 23]
    for t in range(TILES_C):
        part = pl.ds(128 * t, 128)
        tiles2[t] = dense2[0, :, part] + dense2[1, :, part] + dense2[2, :, part]
    sum_scatter(0, tiles2, rs2)

    unit1, inverse1 = norm_parts(feats[...])
    normed1 = (unit1 * gain1).astype(BF16)
    vv[...] = dot_nt(normed1, wt1[2 * WIDE :, :]).astype(BF16)
    kt[...] = dot_nt(wt1[WIDE : 2 * WIDE, :], normed1).astype(BF16)
    queries = dot_nt(normed1, wt1[0:WIDE, :])
    for h in range(HEADS):
        qm[h * CELLS : (h + 1) * CELLS, :] = jnp.where(wide_lane == h, queries, 0.0).astype(BF16)

    drain(mid_recv, mid_in)
    total = lin[12:24, 16:32, :] + mid_in[2].astype(F32).reshape(12, 16, CHANNELS)
    below = (mid_in[0].astype(F32) + mid_in[1].astype(F32)).reshape(12, 16, CHANNELS)
    total = jnp.concatenate([total[0:4], total[4:12] + below[0:8], below[8:12]], axis=0)
    pair = [total[8 * sy : 8 * sy + 8].reshape(8, 1, 16, CHANNELS) for sy in range(2)]
    grad_middle = jnp.concatenate(pair, axis=1).reshape(CELLS, CHANNELS)
    sum_spread(0, tiles2, rs2, ag2)

    grad_in = grad_middle.astype(BF16)
    grads_t = dot_nt(pp1[...], grad_in).astype(BF16)
    grads = dot_nt(grad_in, pp1[...])
    for h in range(HEADS):
        dom[h * CELLS : (h + 1) * CELLS, :] = jnp.where(wide_lane == h, grads, 0.0).astype(BF16)
    for h in range(HEADS):
        half = h // 4 * 128
        probs = p1[:, h * CELLS : (h + 1) * CELLS].astype(F32)
        weighted = probs * dot(vv[:, half : half + 128], head_rows(grads_t, h))
        total = jnp.sum(weighted, axis=0, keepdims=True)
        slopes = weighted - probs * total
        for sx in range(2):

            def group_of(m):
                ky = 15 - m
                return (ky % 8 * 4 + ky // 8 * 2 + sx) * 8

            collect(acc1, h, sx, 16, group_of, slopes)
        slopes_b = slopes.astype(BF16)
        ds1[:, h * CELLS : (h + 1) * CELLS] = slopes_b
        ot[h * HEAD_PAD : (h + 1) * HEAD_PAD, :] = dot(
            kt[h * HEAD_PAD : (h + 1) * HEAD_PAD, :], slopes_b
        )
    sum_gather(0, tiles2, ag2, fin2)

    flat = None
    for s in range(2):
        parts = [
            jnp.concatenate(
                [
                    acc1[s, r].reshape(HEADS * 8, USED_W),
                    jnp.zeros((HEADS * 8, LANES_W - USED_W), F32),
                ],
                axis=1,
            )
            for r in range(4)
        ]
        piece = roll(gather_rows(parts, 1), 15 - 8 * s)
        flat = piece if flat is None else flat + piece
    flat1[...] = flat
    dense1[...] = jnp.zeros(dense1.shape, F32)
    for dy in range(SPAN):
        dense1[0:HEADS, dy * SPAN : (dy + 1) * SPAN] = flat1[:, dy * 32 : dy * 32 + SPAN]
    for t in range(TILES_W):
        tiles1[t] = dense1[:, 128 * t : 128 * t + 128]
    sum_scatter(3, tiles1, rs1)

    grad_queries = (jnp.transpose(ot[...]) * SCALE).astype(BF16)
    grad_keys = (dot(ds1[...], qm[...]) * SCALE).astype(BF16)
    grad_values = dot(p1[...], dom[...])
    grad_first = (
        dot(grad_queries, wt1[0:WIDE, :])
        + dot(grad_keys, wt1[WIDE : 2 * WIDE, :])
        + dot(grad_values.astype(BF16), wt1[2 * WIDE :, :])
    )
    grad_feats = grad_middle + norm_back(unit1, inverse1, gain1, grad_first)
    quarters = grad_feats.reshape(8, 2, 2, 8, CHANNELS)
    backs = []
    for s in (1, 2, 3):
        back_out[s - 1] = quarters[:, s // 2, s % 2].reshape(64, CHANNELS).astype(BF16)
        copy = pltpu.make_async_remote_copy(
            src_ref=back_out.at[s - 1],
            dst_ref=back_in.at[s - 1],
            send_sem=back_send,
            recv_sem=back_recv,
            device_id=at(s // 2, s % 2),
            device_id_type=MESH,
        )
        copy.start()
        backs.append(copy)
    out_ref[8:16, 8:16, :] = quarters[:, 0, 0]
    sum_spread(3, tiles1, rs1, ag1)
    drain(back_recv, back_in)
    out_ref[8:16, 0:8, :] = back_in[0].astype(F32).reshape(8, 8, CHANNELS)
    out_ref[0:8, 8:16, :] = back_in[1].astype(F32).reshape(8, 8, CHANNELS)
    out_ref[0:8, 0:8, :] = back_in[2].astype(F32).reshape(8, 8, CHANNELS)
    sum_gather(3, tiles1, ag1, fin1)
    sum_end(0, tiles2, rs2, ag2, fin2)
    out2_ref[...] = joined(fin2, CROSS * CROSS)
    sum_end(3, tiles1, rs1, ag1, fin1)
    pltpu.make_async_copy(every, every, halo_send).wait()
    drain(mid_send, mid_out)
    drain(back_send, back_out)
    out1_ref[...] = joined(fin1, SPAN * SPAN)


def buffer_plan(tiles, n_lat):
    count = tiles.shape[0]
    chunks = min(n_lat, count)
    return chunks, count // chunks


def body(n_lat, n_lon, *operands):
    vmem = pltpu.VMEM

    def sums(count):
        chunks = min(n_lat, count)
        depth = count // chunks
        return (
            vmem((count, 8, 128), F32),
            vmem((n_lat - 1, depth, 8, 128), F32),
            vmem((n_lon, depth, 8, 128), F32),
            vmem((chunks, depth, 8, 128), F32),
        )

    tiles1, rs1, ag1, fin1 = sums(TILES_W)
    tiles2, rs2, ag2, fin2 = sums(TILES_C)
    scratch = [
        vmem((16, 16, CHANNELS), BF16),
        vmem((16, 16, CHANNELS), BF16),
        vmem((1, CHANNELS), F32),
        vmem((CHANNELS, 3 * CHANNELS), BF16),
        vmem((CHANNELS, CHANNELS), BF16),
        vmem((HEADS, SPAN * SPAN), F32),
        vmem((1, CHANNELS), F32),
        vmem((CHANNELS, 3 * CHANNELS), BF16),
        vmem((CHANNELS, CHANNELS), BF16),
        vmem((HEADS, CROSS * CROSS), F32),
        pltpu.SemaphoreType.DMA((10,)),
        vmem((16, 64, CHANNELS), BF16),
        vmem((HEADS, LANES_W), F32),
        vmem((3, HEADS, LANES_C), F32),
        vmem((3 * WIDE, CHANNELS), BF16),
        vmem((3 * WIDE, CHANNELS), BF16),
        vmem((WIDE, CHANNELS), BF16),
        vmem((WIDE, CHANNELS), BF16),
        vmem((2, CELLS, CELLS), BF16),
        vmem((2, 4, HEADS, 8, USED_W), F32),
        vmem((3, 4, HEADS, 8, USED_C), F32),
        vmem((2, 4, HEADS, 8, USED_W), F32),
        vmem((3, 4, HEADS, 8, USED_C), F32),
        vmem((CELLS, CHANNELS), F32),
        vmem((4, 8, 2, 2, 8, CHANNELS), F32),
        vmem((KEY_SIDE * 32, CHANNELS), F32),
        vmem((KEY_SIDE * 32, 1), F32),
        vmem((CELLS, WIDE), BF16),
        vmem((WIDE, CELLS), BF16),
        vmem((CELLS, WIDE), BF16),
        vmem((WIDE, CELLS), BF16),
        vmem((HEADS * CELLS, WIDE), BF16),
        vmem((HEADS * CELLS, WIDE), BF16),
        vmem((HEADS, 128, CELLS), BF16),
        vmem((HEADS, 128, CELLS), BF16),
        vmem((WIDE, CELLS), F32),
        vmem((CELLS, HEADS * CELLS), BF16),
        vmem((KEYS, HEADS * CELLS), BF16),
        vmem((CELLS, HEADS * CELLS), BF16),
        vmem((KEYS, HEADS * CELLS), BF16),
        vmem((KEYS, WIDE), BF16),
        vmem((KEYS, WIDE), BF16),
        vmem((WIDE, KEYS), BF16),
        vmem((KEY_SIDE, 32, CHANNELS), F32),
        vmem((3, 192, CHANNELS), BF16),
        vmem((3, 192, CHANNELS), BF16),
        vmem((3, 64, CHANNELS), BF16),
        vmem((3, 64, CHANNELS), BF16),
        vmem((8, 128 * TILES_W), F32),
        vmem((3, 8, 128 * TILES_C), F32),
        tiles1,
        tiles2,
        rs1,
        rs2,
        ag1,
        ag2,
        fin1,
        fin2,
        pltpu.SemaphoreType.DMA,
        pltpu.SemaphoreType.DMA,
        pltpu.SemaphoreType.DMA,
        pltpu.SemaphoreType.DMA,
        pltpu.SemaphoreType.DMA,
        pltpu.SemaphoreType.DMA,
        pltpu.SemaphoreType.DMA((6,)),
        pltpu.SemaphoreType.DMA((6,)),
    ]
    whole = pl.BlockSpec(memory_space=pltpu.VMEM)
    return pl.pallas_call(
        functools.partial(kernel, n_lat, n_lon),
        out_shape=(
            jax.ShapeDtypeStruct((16, 16, CHANNELS), F32),
            jax.ShapeDtypeStruct((HEADS, SPAN * SPAN), F32),
            jax.ShapeDtypeStruct((HEADS, CROSS * CROSS), F32),
        ),
        in_specs=[pl.BlockSpec(memory_space=pltpu.HBM)] * 10,
        out_specs=(whole, whole, whole),
        scratch_shapes=scratch,
        compiler_params=pltpu.CompilerParams(
            collective_id=0, has_side_effects=True, vmem_limit_bytes=63 * 1024 * 1024
        ),
    )(*operands)


def solution(mesh):
    def local(
        features,
        cotangent,
        first_gain,
        window_qkv,
        window_proj,
        window_table,
        second_gain,
        cross_qkv,
        cross_proj,
        cross_table,
    ):
        return body(
            mesh.shape["lat"],
            mesh.shape["lon"],
            features,
            cotangent,
            first_gain.reshape(1, CHANNELS),
            window_qkv,
            window_proj,
            window_table,
            second_gain.reshape(1, CHANNELS),
            cross_qkv,
            cross_proj,
            cross_table,
        )

    return jax.shard_map(
        local,
        mesh=mesh,
        in_specs=(
            P("lat", "lon", None),
            P("lat", "lon", None),
            P(),
            P(),
            P(),
            P(),
            P(),
            P(),
            P(),
            P(),
        ),
        out_specs=(P("lat", "lon", None), P(), P()),
        check_vma=False,
    )
```

profile of v0, /device:TPU:1, one launch (start us, length us, event | category | flops | bytes accessed | tf_op | source)
XLA Modules:
  0.0 90.5 jit_solution(17601961344590159280)
XLA Ops:
  0.6 86.7 %shard_map.121 = (f32[16,16,180]{2,1,0:T(8,128)}, f32[6,961]{1,0:T(8,128)}, f32[6,1521]{1,0:T(8,128)}) custom-call(bf16[16,16,180]{2,1,0:T(8,128)(2,1)} %feat_in.1, bf16[16,16,180]{2,1,0:T(8,128)(2,1)} %cot_in_hbm.1, f32[1,180]{1,0:T(1,128)} %bitcast.2, bf16[180,540]{1,0:T(8,128)(2,1)} %qkv1_in.1, bf16[180,180]{1,0:T(8,128)(2,1)} %proj1_in.1, ...), custom_call_target="tpu_custom_call" | custom-call | tf_op jit(solution)/shard_map/pallas_call | solution.py:774
  87.3 0.0 copy-start.1
  87.3 1.7 %copy.16 = f32[16,16,180]{2,1,0:T(8,128)} copy(f32[16,16,180]{2,1,0:T(8,128)} %get-tuple-element.6) | data formatting | bytes 368640
  89.0 0.0 copy-done.1
  89.0 0.0 copy-start
  89.0 0.6 copy.17
  89.6 0.2 copy-done
  89.8 0.6 copy.18
Async XLA Ops:
  87.3 1.7 %copy-start.1 = (f32[6,961]{1,0:T(8,128)S(1)}, f32[6,961]{1,0:T(8,128)}, u32[]{:S(2)}) copy-start(f32[6,961]{1,0:T(8,128)} %get-tuple-element.7) | copy-start | bytes 69196
  89.0 0.8 copy-start
where the time goes:
time: 90.7 us; the launch traced here: 90.5 us
  Pallas kernels  86.7 us (96%)
  local copies, waits for them, and re-layouts  3.11 us (3%)
    pallas_call x1, Pallas kernels, body(): pl.pallas_call(functools.partial(kernel, n_lat, n_lon), out_shape=(jax.Sh...  86.7 us
    unnamed x7, local copies, waits for them, and re-layouts  3.11 us

commit v1 on v0

v1 whole, which is shorter than its diff:
```python
import functools

import jax
import jax.numpy as jnp
from jax import lax
from jax.experimental import pallas as pl
from jax.experimental.pallas import tpu as pltpu
from jax.sharding import PartitionSpec as P

CHANNELS = 180
HEADS = 6
HEAD_SIZE = 30
HEAD_PAD = 32
WIDE = 256
CELLS = 256
KEYS = 576
KEY_SIDE = 24
SPAN = 31
CROSS = 39
EPSILON = 1e-05
NEGATIVE = -1e30
LOG2E = 1.4426950408889634
SCALE = HEAD_SIZE**-0.5
TILES_W = 8
TILES_C = 12
LANES_W = 1024
LANES_C = 1280
USED_W = 640
USED_C = 896
MESH = pl.DeviceIdType.MESH
F32 = jnp.float32
BF16 = jnp.bfloat16


def iota(shape, dim):
    return lax.broadcasted_iota(jnp.int32, shape, dim)


def dot(a, b):
    return jnp.dot(a, b, preferred_element_type=F32)


def dot_nt(a, b):
    return lax.dot_general(a, b, (((1,), (1,)), ((), ())), preferred_element_type=F32)


def one_hot(mask):
    return jnp.where(mask, 1.0, 0.0).astype(BF16)


def roll(x, shift):
    size = x.shape[-1]
    return pltpu.roll(x, shift % size, x.ndim - 1)


def norm_parts(values):
    centre = jnp.mean(values, axis=-1, keepdims=True)
    offset = values - centre
    spread = jnp.mean(offset * offset, axis=-1, keepdims=True)
    inverse = lax.rsqrt(spread + EPSILON)
    return offset * inverse, inverse


def norm_back(unit, inverse, gain, grads):
    scaled = grads * gain
    first = jnp.mean(scaled, axis=-1, keepdims=True)
    second = jnp.mean(scaled * unit, axis=-1, keepdims=True)
    return inverse * (scaled - first - unit * second)


def slot(a, b):
    return (a // 2 * 2 + b // 2) * 4 + a % 2 * 2 + b % 2


OWN = [(sy, sx, 2 * sy + sx, (1 - sy) * 2 + (1 - sx)) for sy in (0, 1) for sx in (0, 1)]


def spread_rows(base, stride, ways):
    rows = iota(base.shape, 0)
    for bit in (1, 2, 4):
        base = jnp.where((rows & bit) != 0, roll(base, stride * bit), base)
    upper = (iota(base.shape, 1) & 16) != 0
    base = jnp.where(upper, roll(base, -240), base)
    return [base if r == 0 else roll(base, -32 * r) for r in range(ways)]


def gather_rows(parts, stride):
    total = parts[0]
    for r in range(1, len(parts)):
        total = total + roll(parts[r], 32 * r)
    upper = (iota(total.shape, 1) & 16) != 0
    total = jnp.where(upper, 0.0, total) + roll(jnp.where(upper, total, 0.0), 240)
    rows = iota(total.shape, 0)
    for bit in (1, 2, 4):
        total = jnp.where((rows & bit) != 0, roll(total, -stride * bit), total)
    return jnp.sum(total, axis=0, keepdims=True)


def kernel(
    n_lat,
    n_lon,
    feat_in,
    cot_in_hbm,
    gain1_in,
    qkv1_in,
    proj1_in,
    tab1_in,
    gain2_in,
    qkv2_in,
    proj2_in,
    tab2_in,
    out_ref,
    out1_ref,
    out2_ref,
    feat_ref,
    cot_ref,
    gain1_ref,
    qkv1_ref,
    proj1_ref,
    tab1_ref,
    gain2_ref,
    qkv2_ref,
    proj2_ref,
    tab2_ref,
    load_sem,
    region,
    flat1,
    flat2,
    wt1,
    wt2,
    pp1,
    pp2,
    turn,
    z1,
    z2,
    acc1,
    acc2,
    feats,
    middles,
    units,
    inverses,
    kk,
    vt,
    vv,
    kt,
    qm,
    dom,
    qmt,
    gt,
    ot,
    normed,
    inverse1,
    s1,
    s2,
    g2,
    grad_mid,
    grad_first,
    p1,
    p2,
    ds1,
    ds2,
    k2,
    v2,
    k2t,
    lin,
    mid_out,
    mid_in,
    back_out,
    back_in,
    dense1,
    dense2,
    tiles1,
    tiles2,
    rs1,
    rs2,
    ag1,
    ag2,
    far1,
    far2,
    fin1,
    fin2,
    halo_send,
    halo_recv,
    mid_send,
    mid_recv,
    back_send,
    back_recv,
    sum_send,
    sum_recv,
):
    lat = lax.axis_index("lat")
    lon = lax.axis_index("lon")

    def wrapped(value, count):
        value = jnp.where(value >= count, value - count, value)
        return jnp.where(value < 0, value + count, value)

    def at(dy, dx):
        return (wrapped(lon + dx, n_lon), wrapped(lat + dy, n_lat))

    loads = [
        pltpu.make_async_copy(src, dst, load_sem.at[i])
        for i, (src, dst) in enumerate(
            (
                (feat_in, feat_ref),
                (qkv1_in, qkv1_ref),
                (proj1_in, proj1_ref),
                (qkv2_in, qkv2_ref),
                (proj2_in, proj2_ref),
                (tab1_in, tab1_ref),
                (tab2_in, tab2_ref),
                (gain1_in, gain1_ref),
                (gain2_in, gain2_ref),
                (cot_in_hbm, cot_ref),
            )
        )
    ]
    for load in loads:
        load.start()

    barrier = pltpu.get_barrier_semaphore()

    def greet(dy, dx):
        pl.semaphore_signal(barrier, inc=1, device_id=at(dy, dx), device_id_type=MESH)

    for dy in (-1, 1):
        for dx in (-1, 1):
            greet(dy, dx)
    for j in range(1, n_lat):
        greet(j, 0)
    greet(0, 1)
    greet(0, -1)
    inner, outer = lon_plan(n_lon)
    spot = lax.rem(lon, inner)

    def inner_peer(j):
        return (lon - spot + wrapped(spot + j, inner), lat)

    def greet_at(device):
        pl.semaphore_signal(barrier, inc=1, device_id=device, device_id_type=MESH)

    for j in range(1, inner):
        greet_at(inner_peer(j))
    for j in range(1, outer):
        greet(0, j * inner)

    loads[0].wait()
    own = feat_ref[...].astype(F32)
    for sy, sx, w, s in OWN:
        quarter = own[8 * sy : 8 * sy + 8, 8 * sx : 8 * sx + 8, :].reshape(64, CHANNELS)
        region[w * 4 + s] = quarter.astype(BF16)

    for load in loads[1:7]:
        load.wait()

    def pad_weights(i, _):
        lane = iota((WIDE, 1), 0)
        real = (lane < 192) & ((lane & 31) < HEAD_SIZE)
        source = jnp.where(real, CHANNELS * i + lane - 2 * (lane >> 5), -1)
        pick = one_hot(iota((WIDE, 3 * CHANNELS), 1) == source)
        rows = pl.ds(pl.multiple_of(i * WIDE, WIDE), WIDE)
        wt1[rows, :] = dot_nt(pick, qkv1_ref[...]).astype(BF16)
        wt2[rows, :] = dot_nt(pick, qkv2_ref[...]).astype(BF16)

        @pl.when(i == 0)
        def _():
            pick_proj = pick[:, :CHANNELS]
            pp1[...] = dot(pick_proj, proj1_ref[...]).astype(BF16)
            pp2[...] = dot(pick_proj, proj2_ref[...]).astype(BF16)

        return 0

    lax.fori_loop(0, 3, pad_weights, 0)

    pl.semaphore_wait(barrier, 4 + 2 + n_lat - 1 + inner - 1 + outer - 1)

    halo = []
    for a in (1, 2):
        for b in (1, 2):
            for dy in (0, -1 if a == 1 else 1):
                for dx in (0, -1 if b == 1 else 1):
                    if dy == 0 and dx == 0:
                        continue
                    halo.append(
                        pltpu.make_async_remote_copy(
                            src_ref=region.at[slot(a, b)],
                            dst_ref=region.at[slot(a - 2 * dy, b - 2 * dx)],
                            send_sem=halo_send,
                            recv_sem=halo_recv,
                            device_id=at(dy, dx),
                            device_id_type=MESH,
                        )
                    )
    for copy in halo:
        copy.start()

    for load in loads[7:]:
        load.wait()

    def turned(c):
        r = 255 - c
        return ((r >> 3) & 7) * 32 + ((r >> 7) & 1) * 16 + ((r >> 6) & 1) * 8 + (r & 7)

    turn[0] = one_hot(iota((CELLS, CELLS), 0) == turned(iota((1, CELLS), 1)))
    turn[1] = one_hot(iota((CELLS, CELLS), 1) == turned(iota((CELLS, 1), 0)))

    flat1[...] = jnp.zeros(flat1.shape, F32)
    flat2[...] = jnp.zeros(flat2.shape, F32)
    for dy in range(SPAN):
        flat1[:, dy * 32 : dy * 32 + SPAN] = tab1_ref[:, dy * SPAN : (dy + 1) * SPAN]
    for dy in range(CROSS):
        for s in range(3):
            start = dy * CROSS + 8 * s
            flat2[s, :, dy * 32 : dy * 32 + 23] = tab2_ref[:, start : start + 23]
    def spread(pair, _):
        for i in range(2):
            h = 2 * pair + i
            row = pl.ds(h, 1)
            for s in range(2):
                base = jnp.broadcast_to(flat1[row, :] * LOG2E, (8, LANES_W))
                for r, part in enumerate(spread_rows(roll(base, 8 * s - 15), 1, 4)):
                    z1[s, r, h] = part[:, :USED_W]
            for s in range(3):
                base = jnp.broadcast_to(flat2[s, row, :] * LOG2E, (8, LANES_C))
                for r, part in enumerate(spread_rows(base, -1, 4)):
                    z2[s, r, h] = part[:, :USED_C]
        return 0

    lax.fori_loop(0, HEADS // 2, spread, 0)
    query_half = (iota((1, CELLS), 1) >> 4) & 1

    def window_bias(h, y8):
        pieces = []
        for sy in range(2):
            t, r = divmod(15 - (8 * sy + y8), 4)
            for sx in range(2):
                pieces.append(z1[sx, r, h, :, 128 * t : 128 * t + CELLS])
        return jnp.concatenate(pieces, axis=0)

    def cross_bias(h, ky):
        t, r = divmod(ky, 4)
        pieces = [z2[s, r, h, :, 128 * t : 128 * t + CELLS] for s in range(3)]
        return jnp.concatenate(pieces, axis=0)

    def by_eight(values):
        return values.reshape(values.shape[0] // 8, 8, CELLS)

    def add_bias(scores, step, count, bias):
        peak = None
        for c in range(count):
            rows = slice(c * step, (c + 1) * step)
            part = scores[rows, :] * (SCALE * LOG2E) + bias(c)
            scores[rows, :] = part
            part = jnp.max(by_eight(part), axis=0)
            peak = part if peak is None else jnp.maximum(peak, part)
        return jnp.max(peak, axis=0, keepdims=True)

    def raise_all(scores, step, count, peak, probs, columns, keep):
        total = None
        for c in range(count):
            rows = slice(c * step, (c + 1) * step)
            part = jnp.exp2(scores[rows, :] - peak)
            probs[rows, columns] = part.astype(BF16)
            if keep:
                scores[rows, :] = part
            part = jnp.sum(by_eight(part), axis=0)
            total = part if total is None else total + part
        return 1.0 / jnp.sum(total, axis=0, keepdims=True)

    def weigh_all(raised, grads, step, count, inverse):
        total = None
        for c in range(count):
            rows = slice(c * step, (c + 1) * step)
            part = raised(rows) * grads[rows, :]
            grads[rows, :] = part
            part = jnp.sum(by_eight(part), axis=0)
            total = part if total is None else total + part
        return jnp.sum(total, axis=0, keepdims=True) * inverse

    def slope_all(raised, grads, step, count, total, slopes, packed, columns):
        for c in range(count):
            rows = slice(c * step, (c + 1) * step)
            part = grads[rows, :] - raised(rows) * total
            slopes[rows, :] = part
            packed[rows, columns] = part.astype(BF16)

    def collect(acc, h, s, count, group_of, slopes):
        for r in range(4):
            for t in range(count // 4 + 1):
                parts = []
                if t < count // 4:
                    group = group_of(4 * t + r)
                    parts.append(slopes[group : group + 8, 0:128])
                if t > 0:
                    group = group_of(4 * t - 4 + r)
                    parts.append(slopes[group : group + 8, 128:256])
                acc[s, r, h, :, 128 * t : 128 * t + 128] = sum(parts[1:], parts[0])

    def head_rows(rows, h):
        before = h % 4 * HEAD_PAD
        pieces = [rows]
        if before:
            pieces = [jnp.zeros((before, CELLS), rows.dtype)] + pieces
        if before + HEAD_PAD < 128:
            pieces.append(jnp.zeros((128 - HEAD_PAD - before, CELLS), rows.dtype))
        return jnp.concatenate(pieces, axis=0) if len(pieces) > 1 else rows

    def head_block(rows, h):
        four = jnp.concatenate([rows] * 4, axis=0)
        return jnp.where((iota((128, CELLS), 0) >> 5) == lax.rem(h, 4), four, 0.0).astype(BF16)

    def head_lanes(values, into):
        zeros = jnp.zeros((CELLS, 128), BF16)
        for h in range(HEADS):
            half = h // 4 * 128
            lanes = iota((CELLS, 128), 1) >> 5
            own_lanes = jnp.where(lanes == h % 4, values[:, half : half + 128], 0.0).astype(BF16)
            rows = slice(h * CELLS, (h + 1) * CELLS)
            into[rows, half : half + 128] = own_lanes
            into[rows, 128 - half : 256 - half] = zeros

    every = region.at[pl.ds(0, 12)]
    pltpu.make_async_copy(every, every, halo_recv).wait()

    gain1 = gain1_ref[...]
    gain2 = gain2_ref[...]

    key_half = 30 + ((iota((CELLS, 1), 0) >> 4) & 1)
    lane_row = iota((1, WIDE), 1)
    marks = key_half == jnp.where(lane_row < 192, lane_row & 31, 0)
    pad_row = iota((HEAD_PAD, CELLS), 0)

    def own_columns(h):
        return slice(h * CELLS, (h + 1) * CELLS)

    def own_rows(h):
        return slice(h * HEAD_PAD, (h + 1) * HEAD_PAD)

    def window_row(wy, _):
        for wx in range(2):
            w = 2 * wy + wx
            for c in range(4):
                parts = [
                    region[w * 4 + s, 16 * c : 16 * c + 16, :]
                    .astype(F32)
                    .reshape(2, 1, 8, CHANNELS)
                    for s in range(4)
                ]
                values = jnp.concatenate(parts, axis=1).reshape(64, CHANNELS)
                rows = slice(64 * c, 64 * c + 64)
                feats[wx, rows, :] = values
                unit, _ = norm_parts(values)
                normed[wx, rows, :] = (unit * gain1).astype(BF16)
        edge = lat == jnp.where(wy == 0, 0, n_lat - 1)
        floor = jnp.where(edge, NEGATIVE, 0.0)
        hidden = jnp.where(pad_row - 30 == 1 - query_half, floor, 0.0)
        hidden = jnp.where(pad_row >= 30, hidden, 0.0)
        for wx in range(2):
            queries = dot_nt(wt1[0:WIDE, :], normed[wx])
            for h in range(HEADS):
                qmt[wx, h] = head_rows((queries[own_rows(h), :] + hidden).astype(BF16), h)
            keys = dot_nt(normed[wx], wt1[WIDE : 2 * WIDE, :])
            kk[wx] = jnp.where(marks, 1.0, keys).astype(BF16)
            vt[wx] = dot_nt(wt1[2 * WIDE :, :], normed[wx]).astype(BF16)
        for wx in range(2):
            for h in range(HEADS):
                half = h // 4 * 128
                s1[wx, h] = dot(kk[wx, :, half : half + 128], qmt[wx, h])
        for wx in range(2):
            for h in range(HEADS):
                scores = s1.at[wx, h]
                peak = add_bias(scores, 32, 8, functools.partial(window_bias, h))
                inverse = raise_all(scores, 32, 8, peak, p1.at[wx], own_columns(h), False)
                inverse1[wx, h] = inverse
        for wx in range(2):
            for h in range(HEADS):
                rows = own_rows(h)
                heads_t = dot(vt[wx, rows, :], p1[wx, :, own_columns(h)])
                ot[wx, rows, :] = heads_t * inverse1[wx, h]
        for wx in range(2):
            heads_out = jnp.transpose(ot[wx]).astype(BF16)
            middle = feats[wx] + dot(heads_out, pp1[...])
            middles[2 * wy + wx] = middle.reshape(8, 2, 2, 8, CHANNELS)
        return 0

    ot[...] = jnp.zeros(ot.shape, F32)
    lax.fori_loop(0, 2, window_row, 0)

    y_runs = ((0, 0, 4, 8, 0), (0, 1, 0, 8, 4), (1, 0, 0, 8, 12), (1, 1, 0, 4, 20))
    for wy, sy, first, last, place in y_runs:
        for wx in range(2):
            for sx in range(2):
                start = (2 * wx + sx) * 8
                lin[place : place + last - first, start : start + 8, :] = middles[
                    2 * wy + wx, first:last, sy, sx
                ]

    def second_norm(step, _):
        for k in range(4):
            i = 4 * step + k
            lines, rows = pl.ds(2 * i, 2), pl.ds(pl.multiple_of(64 * i, 64), 64)
            unit, inverse = norm_parts(lin[lines].reshape(64, CHANNELS))
            units[rows, :] = unit
            inverses[rows, :] = inverse
            normal = (unit * gain2).astype(BF16).astype(F32)
            lin[lines] = normal.reshape(2, 32, CHANNELS)
        return 0

    lax.fori_loop(0, KEY_SIDE // 8, second_norm, 0)
    inside_low = jnp.where(lat > 0, 1.0, 0.0)
    inside_high = jnp.where(lat < n_lat - 1, 1.0, 0.0)
    lin[0:4] = lin[0:4] * inside_low
    lin[20:24] = lin[20:24] * inside_high
    keys_in = lin[:, 4:28, :].reshape(KEYS, CHANNELS).astype(BF16)
    k2[...] = dot_nt(keys_in, wt2[WIDE : 2 * WIDE, :]).astype(BF16)
    v2[...] = dot_nt(keys_in, wt2[2 * WIDE :, :]).astype(BF16)
    k2t[...] = dot_nt(wt2[WIDE : 2 * WIDE, :], keys_in).astype(BF16)

    def own_part(sy, sx):
        return slice(4 + 8 * sy, 12 + 8 * sy), slice(8 + 8 * sx, 16 + 8 * sx)

    own_second = jnp.concatenate(
        [lin[(*own_part(sy, sx), slice(None))].reshape(64, CHANNELS) for sy, sx, w, s in OWN],
        axis=0,
    )
    queries_in = dot(turn[0], own_second.astype(BF16)).astype(BF16)
    cot = cot_ref[...].astype(F32)
    cot_own = [
        cot[8 * sy : 8 * sy + 8, 8 * sx : 8 * sx + 8, :].reshape(64, CHANNELS)
        for sy, sx, w, s in OWN
    ]
    cot_in = dot(turn[0], jnp.concatenate(cot_own, axis=0).astype(BF16)).astype(BF16)
    queries_t = dot_nt(wt2[0:WIDE, :], queries_in).astype(BF16)
    gt[...] = dot_nt(pp2[...], cot_in)
    for h in range(HEADS):
        qmt[0, h] = head_rows(queries_t[h * HEAD_PAD : (h + 1) * HEAD_PAD, :], h)
    head_lanes(dot_nt(queries_in, wt2[0:WIDE, :]), qm)

    def cross_heads(group, _):
        heads = [3 * group + i for i in range(3)]

        def half(h):
            return pl.ds(pl.multiple_of(h // 4 * 128, 128), 128)

        def columns(h):
            return pl.ds(pl.multiple_of(h * CELLS, CELLS), CELLS)

        def rows(h):
            return pl.ds(pl.multiple_of(h * HEAD_PAD, HEAD_PAD), HEAD_PAD)

        def bias(h, c):
            return jnp.concatenate([cross_bias(h, 2 * c), cross_bias(h, 2 * c + 1)], axis=0)

        for i, h in enumerate(heads):
            s2[i] = dot(k2[:, half(h)], qmt[0, h])
        inverse = []
        for i, h in enumerate(heads):
            peak = add_bias(s2.at[i], 48, 12, functools.partial(bias, h))
            inverse.append(raise_all(s2.at[i], 48, 12, peak, p2, columns(h), True))
            scaled = gt[rows(h), :] * inverse[i]
            gt[rows(h), :] = scaled
            g2[i] = dot(v2[:, half(h)], head_block(scaled, h))
        for i, h in enumerate(heads):
            scores, grads = s2.at[i], g2.at[i]

            def raised(part):
                return scores[part, :]

            total = weigh_all(raised, grads, 48, 12, inverse[i])
            slope_all(raised, grads, 48, 12, total, scores, ds2, columns(h))
            for s in range(3):
                collect(acc2, h, s, KEY_SIDE, lambda m: (m * 3 + s) * 8, scores)
        for h in heads:
            ot[0, rows(h), :] = dot(k2t[rows(h), :], ds2[:, columns(h)])
        return 0

    lax.fori_loop(0, HEADS // 3, cross_heads, 0)
    head_lanes(jnp.transpose(gt[...]), dom)
    grad_queries = (jnp.transpose(ot[0]) * SCALE).astype(BF16)
    grad_keys = (dot(ds2[...], qm[...]) * SCALE).astype(BF16)
    grad_values = dot(p2[...], dom[...]).astype(BF16)
    grad_second = dot(grad_keys, wt2[WIDE : 2 * WIDE, :]) + dot(grad_values, wt2[2 * WIDE :, :])
    grad_own = dot(turn[1], dot(grad_queries, wt2[0:WIDE, :]).astype(BF16))

    lin[...] = jnp.zeros(lin.shape, F32)
    lin[:, 4:28, :] = grad_second.reshape(KEY_SIDE, KEY_SIDE, CHANNELS)
    lin[0:4] = lin[0:4] * inside_low
    lin[20:24] = lin[20:24] * inside_high
    for i, (sy, sx, w, s) in enumerate(OWN):
        place = (*own_part(sy, sx), slice(None))
        lin[place] = lin[place] + grad_own[64 * i : 64 * i + 64, :].reshape(8, 8, CHANNELS)

    def second_back(step, _):
        for k in range(4):
            i = 4 * step + k
            lines, rows = pl.ds(2 * i, 2), pl.ds(pl.multiple_of(64 * i, 64), 64)
            grad = lin[lines].reshape(64, CHANNELS)
            grad = norm_back(units[rows, :], inverses[rows, :], gain2, grad)
            lin[lines] = grad.reshape(2, 32, CHANNELS)
        return 0

    lax.fori_loop(0, KEY_SIDE // 8, second_back, 0)
    for i, (sy, sx, w, s) in enumerate(OWN):
        place = (*own_part(sy, sx), slice(None))
        lin[place] = lin[place] + cot_own[i].reshape(8, 8, CHANNELS)
    for w in range(3):
        rows, cols = 12 * (w // 2), 16 * (w % 2)
        piece = lin[rows : rows + 12, cols : cols + 16, :]
        mid_out[w] = piece.reshape(192, CHANNELS).astype(BF16)
        pltpu.make_async_remote_copy(
            src_ref=mid_out.at[w],
            dst_ref=mid_in.at[w],
            send_sem=mid_send,
            recv_sem=mid_recv,
            device_id=at(w // 2 - 1, w % 2 - 1),
            device_id_type=MESH,
        ).start()

    def sum_scatter(kind, tiles, buffer):
        chunks, depth = buffer_plan(tiles, n_lat)
        for c in range(chunks):

            @pl.when(lat != c)
            def _():
                pltpu.make_async_remote_copy(
                    src_ref=tiles.at[pl.ds(c * depth, depth)],
                    dst_ref=buffer.at[wrapped(lat - c, n_lat) - 1],
                    send_sem=sum_send.at[kind],
                    recv_sem=sum_recv.at[kind],
                    device_id=(lon, c),
                    device_id_type=MESH,
                ).start()

    def drain(sem, ref):
        pltpu.make_async_copy(ref, ref, sem).wait()

    def sum_spread(kind, tiles, buffer, rows):
        chunks, depth = buffer_plan(tiles, n_lat)

        @pl.when(lat < chunks)
        def _():
            drain(sum_recv.at[kind], buffer)
            total = tiles[pl.ds(lat * depth, depth)]
            for i in range(n_lat - 1):
                total = total + buffer[i]
            rows[spot] = total
            for j in range(1, inner):
                pltpu.make_async_remote_copy(
                    src_ref=rows.at[spot],
                    dst_ref=rows.at[spot],
                    send_sem=sum_send.at[kind + 1],
                    recv_sem=sum_recv.at[kind + 1],
                    device_id=inner_peer(j),
                    device_id_type=MESH,
                ).start()

    def sum_cross(kind, tiles, rows, far):
        chunks, depth = buffer_plan(tiles, n_lat)
        block = lax.div(lon, inner)

        @pl.when(lat < chunks)
        def _():
            drain(sum_recv.at[kind + 1], rows.at[pl.ds(0, inner - 1)])
            total = rows[0]
            for i in range(1, inner):
                total = total + rows[i]
            far[block] = total
            for j in range(1, outer):
                pltpu.make_async_remote_copy(
                    src_ref=far.at[block],
                    dst_ref=far.at[block],
                    send_sem=sum_send.at[kind + 2],
                    recv_sem=sum_recv.at[kind + 2],
                    device_id=at(0, j * inner),
                    device_id_type=MESH,
                ).start()

    def sum_gather(kind, tiles, far, result):
        chunks, depth = buffer_plan(tiles, n_lat)

        @pl.when(lat < chunks)
        def _():
            if outer > 1:
                drain(sum_recv.at[kind + 2], far.at[pl.ds(0, outer - 1)])
            total = far[0]
            for i in range(1, outer):
                total = total + far[i]
            result[lat] = total
            for j in range(1, n_lat):
                pltpu.make_async_remote_copy(
                    src_ref=result.at[lat],
                    dst_ref=result.at[lat],
                    send_sem=sum_send.at[kind + 3],
                    recv_sem=sum_recv.at[kind + 3],
                    device_id=at(j, 0),
                    device_id_type=MESH,
                ).start()

    def sum_end(kind, tiles, buffer, rows, far, result):
        chunks, depth = buffer_plan(tiles, n_lat)

        @pl.when(lat < chunks)
        def _():
            if chunks > 1:
                drain(sum_recv.at[kind + 3], result.at[pl.ds(0, chunks - 1)])
                drain(sum_send.at[kind], result.at[pl.ds(0, chunks - 1)])
            drain(sum_send.at[kind + 1], rows.at[pl.ds(0, inner - 1)])
            if outer > 1:
                drain(sum_send.at[kind + 2], far.at[pl.ds(0, outer - 1)])
            drain(sum_send.at[kind + 3], buffer)

        @pl.when(lat >= chunks)
        def _():
            drain(sum_recv.at[kind + 3], result)
            drain(sum_send.at[kind], result)

    def joined(result, count):
        chunks, depth = result.shape[0], result.shape[1]
        whole = jnp.concatenate(
            [result[c, d] for c in range(chunks) for d in range(depth)], axis=1
        )
        return whole[:, :count]

    def widened(part, width):
        return jnp.concatenate([part, jnp.zeros((8, width - part.shape[1]), F32)], axis=1)

    def gather_cross(pair, _):
        for i in range(2):
            h = 2 * pair + i
            for s in range(3):
                parts = [widened(acc2[s, r, h], LANES_C) for r in range(4)]
                flat2[s, pl.ds(h, 1), :] = gather_rows(parts, -1)
        return 0

    lax.fori_loop(0, HEADS // 2, gather_cross, 0)
    dense2[...] = jnp.zeros(dense2.shape, F32)
    for dy in range(CROSS):
        for s in range(3):
            start = dy * CROSS + 8 * s
            dense2[s, 0:HEADS, start : start + 23] = flat2[s, :, dy * 32 : dy * 32 + 23]
    for t in range(TILES_C):
        part = pl.ds(128 * t, 128)
        whole = dense2[0, :, part] + dense2[1, :, part] + dense2[2, :, part]
        tiles2[t] = whole[:HEADS]
    sum_scatter(0, tiles2, rs2)

    vv[...] = dot_nt(normed[1], wt1[2 * WIDE :, :]).astype(BF16)
    kt[...] = dot_nt(wt1[WIDE : 2 * WIDE, :], normed[1]).astype(BF16)
    head_lanes(dot_nt(normed[1], wt1[0:WIDE, :]), qm)

    drain(mid_recv, mid_in)
    total = lin[12:24, 16:32, :] + mid_in[2].astype(F32).reshape(12, 16, CHANNELS)
    below = (mid_in[0].astype(F32) + mid_in[1].astype(F32)).reshape(12, 16, CHANNELS)
    total = jnp.concatenate([total[0:4], total[4:12] + below[0:8], below[8:12]], axis=0)
    pair = [total[8 * sy : 8 * sy + 8].reshape(8, 1, 16, CHANNELS) for sy in range(2)]
    grad_mid[...] = jnp.concatenate(pair, axis=1).reshape(CELLS, CHANNELS)
    sum_spread(0, tiles2, rs2, ag2)

    grads_t = dot_nt(pp1[...], grad_mid[...].astype(BF16))
    for h in range(HEADS):
        scaled = grads_t[own_rows(h), :] * inverse1[1, h]
        gt[own_rows(h), :] = scaled
        half = h // 4 * 128
        s1[1, h] = dot(vv[:, half : half + 128], head_rows(scaled.astype(BF16), h))
    for h in range(HEADS):

        def raised(part):
            return p1[1, part, own_columns(h)].astype(F32)

        total = weigh_all(raised, s1.at[1, h], 32, 8, inverse1[1, h])
        slope_all(raised, s1.at[1, h], 32, 8, total, s1.at[0, h], ds1, own_columns(h))
        for sx in range(2):

            def group_of(m):
                ky = 15 - m
                return (ky % 8 * 4 + ky // 8 * 2 + sx) * 8

            collect(acc1, h, sx, 16, group_of, s1.at[0, h])
    sum_cross(0, tiles2, ag2, far2)

    for h in range(HEADS):
        total = None
        for s in range(2):
            parts = [widened(acc1[s, r, h], LANES_W) for r in range(4)]
            piece = roll(gather_rows(parts, 1), 15 - 8 * s)
            total = piece if total is None else total + piece
        flat1[h : h + 1, :] = total
    dense1[...] = jnp.zeros(dense1.shape, F32)
    for dy in range(SPAN):
        dense1[0:HEADS, dy * SPAN : (dy + 1) * SPAN] = flat1[:, dy * 32 : dy * 32 + SPAN]
    for t in range(TILES_W):
        tiles1[t] = dense1[:HEADS, 128 * t : 128 * t + 128]
    sum_scatter(4, tiles1, rs1)
    sum_gather(0, tiles2, far2, fin2)

    for h in range(HEADS):
        ot[0, own_rows(h), :] = dot(kt[own_rows(h), :], ds1[:, own_columns(h)])
    head_lanes(jnp.transpose(gt[...]), dom)
    grad_queries = (jnp.transpose(ot[0]) * SCALE).astype(BF16)
    grad_keys = (dot(ds1[...], qm[...]) * SCALE).astype(BF16)
    grad_values = dot(p1[1], dom[...])
    grad_first[...] = (
        dot(grad_queries, wt1[0:WIDE, :])
        + dot(grad_keys, wt1[WIDE : 2 * WIDE, :])
        + dot(grad_values.astype(BF16), wt1[2 * WIDE :, :])
    )
    for c in range(4):
        rows = slice(64 * c, 64 * c + 64)
        unit, inverse = norm_parts(feats[1, rows, :])
        grad = grad_mid[rows, :] + norm_back(unit, inverse, gain1, grad_first[rows, :])
        quarters = grad.reshape(2, 2, 2, 8, CHANNELS)
        out_ref[8 + 2 * c : 10 + 2 * c, 8:16, :] = quarters[:, 0, 0]
        for s in (1, 2, 3):
            piece = quarters[:, s // 2, s % 2].reshape(16, CHANNELS)
            back_out[s - 1, 16 * c : 16 * c + 16, :] = piece.astype(BF16)
    for s in (1, 2, 3):
        pltpu.make_async_remote_copy(
            src_ref=back_out.at[s - 1],
            dst_ref=back_in.at[s - 1],
            send_sem=back_send,
            recv_sem=back_recv,
            device_id=at(s // 2, s % 2),
            device_id_type=MESH,
        ).start()
    sum_spread(4, tiles1, rs1, ag1)
    drain(back_recv, back_in)
    out_ref[8:16, 0:8, :] = back_in[0].astype(F32).reshape(8, 8, CHANNELS)
    out_ref[0:8, 8:16, :] = back_in[1].astype(F32).reshape(8, 8, CHANNELS)
    out_ref[0:8, 0:8, :] = back_in[2].astype(F32).reshape(8, 8, CHANNELS)
    sum_cross(4, tiles1, ag1, far1)
    sum_gather(4, tiles1, far1, fin1)
    sum_end(0, tiles2, rs2, ag2, far2, fin2)
    out2_ref[...] = joined(fin2, CROSS * CROSS)
    sum_end(4, tiles1, rs1, ag1, far1, fin1)
    pltpu.make_async_copy(every, every, halo_send).wait()
    drain(mid_send, mid_out)
    drain(back_send, back_out)
    out1_ref[...] = joined(fin1, SPAN * SPAN)


def lon_plan(n_lon):
    inner = 8 if n_lon % 8 == 0 else 2 if n_lon % 2 == 0 else n_lon
    return inner, n_lon // inner


def buffer_plan(tiles, n_lat):
    count = tiles.shape[0]
    chunks = min(n_lat, count)
    return chunks, count // chunks


def body(n_lat, n_lon, *operands):
    vmem = pltpu.VMEM
    inner, outer = lon_plan(n_lon)

    def sums(count):
        chunks = min(n_lat, count)
        depth = count // chunks
        return (
            vmem((count, HEADS, 128), F32),
            vmem((n_lat - 1, depth, HEADS, 128), F32),
            vmem((inner, depth, HEADS, 128), F32),
            vmem((outer, depth, HEADS, 128), F32),
            vmem((chunks, depth, HEADS, 128), F32),
        )

    tiles1, rs1, ag1, far1, fin1 = sums(TILES_W)
    tiles2, rs2, ag2, far2, fin2 = sums(TILES_C)
    scratch = [
        vmem((16, 16, CHANNELS), BF16),
        vmem((16, 16, CHANNELS), BF16),
        vmem((1, CHANNELS), F32),
        vmem((CHANNELS, 3 * CHANNELS), BF16),
        vmem((CHANNELS, CHANNELS), BF16),
        vmem((HEADS, SPAN * SPAN), F32),
        vmem((1, CHANNELS), F32),
        vmem((CHANNELS, 3 * CHANNELS), BF16),
        vmem((CHANNELS, CHANNELS), BF16),
        vmem((HEADS, CROSS * CROSS), F32),
        pltpu.SemaphoreType.DMA((10,)),
        vmem((16, 64, CHANNELS), BF16),
        vmem((HEADS, LANES_W), F32),
        vmem((3, HEADS, LANES_C), F32),
        vmem((3 * WIDE, CHANNELS), BF16),
        vmem((3 * WIDE, CHANNELS), BF16),
        vmem((WIDE, CHANNELS), BF16),
        vmem((WIDE, CHANNELS), BF16),
        vmem((2, CELLS, CELLS), BF16),
        vmem((2, 4, HEADS, 8, USED_W), F32),
        vmem((3, 4, HEADS, 8, USED_C), F32),
        vmem((2, 4, HEADS, 8, USED_W), F32),
        vmem((3, 4, HEADS, 8, USED_C), F32),
        vmem((2, CELLS, CHANNELS), F32),
        vmem((4, 8, 2, 2, 8, CHANNELS), F32),
        vmem((KEY_SIDE * 32, CHANNELS), F32),
        vmem((KEY_SIDE * 32, 1), F32),
        vmem((2, CELLS, WIDE), BF16),
        vmem((2, WIDE, CELLS), BF16),
        vmem((CELLS, WIDE), BF16),
        vmem((WIDE, CELLS), BF16),
        vmem((HEADS * CELLS, WIDE), BF16),
        vmem((HEADS * CELLS, WIDE), BF16),
        vmem((2, HEADS, 128, CELLS), BF16),
        vmem((WIDE, CELLS), F32),
        vmem((2, WIDE, CELLS), F32),
        vmem((2, CELLS, CHANNELS), BF16),
        vmem((2, HEADS, 1, CELLS), F32),
        vmem((2, HEADS, CELLS, CELLS), F32),
        vmem((3, KEYS, CELLS), F32),
        vmem((3, KEYS, CELLS), F32),
        vmem((CELLS, CHANNELS), F32),
        vmem((CELLS, CHANNELS), F32),
        vmem((2, CELLS, HEADS * CELLS), BF16),
        vmem((KEYS, HEADS * CELLS), BF16),
        vmem((CELLS, HEADS * CELLS), BF16),
        vmem((KEYS, HEADS * CELLS), BF16),
        vmem((KEYS, WIDE), BF16),
        vmem((KEYS, WIDE), BF16),
        vmem((WIDE, KEYS), BF16),
        vmem((KEY_SIDE, 32, CHANNELS), F32),
        vmem((3, 192, CHANNELS), BF16),
        vmem((3, 192, CHANNELS), BF16),
        vmem((3, 64, CHANNELS), BF16),
        vmem((3, 64, CHANNELS), BF16),
        vmem((8, 128 * TILES_W), F32),
        vmem((3, 8, 128 * TILES_C), F32),
        tiles1,
        tiles2,
        rs1,
        rs2,
        ag1,
        ag2,
        far1,
        far2,
        fin1,
        fin2,
        pltpu.SemaphoreType.DMA,
        pltpu.SemaphoreType.DMA,
        pltpu.SemaphoreType.DMA,
        pltpu.SemaphoreType.DMA,
        pltpu.SemaphoreType.DMA,
        pltpu.SemaphoreType.DMA,
        pltpu.SemaphoreType.DMA((8,)),
        pltpu.SemaphoreType.DMA((8,)),
    ]
    whole = pl.BlockSpec(memory_space=pltpu.VMEM)
    return pl.pallas_call(
        functools.partial(kernel, n_lat, n_lon),
        out_shape=(
            jax.ShapeDtypeStruct((16, 16, CHANNELS), F32),
            jax.ShapeDtypeStruct((HEADS, SPAN * SPAN), F32),
            jax.ShapeDtypeStruct((HEADS, CROSS * CROSS), F32),
        ),
        in_specs=[pl.BlockSpec(memory_space=pltpu.HBM)] * 10,
        out_specs=(whole, whole, whole),
        scratch_shapes=scratch,
        compiler_params=pltpu.CompilerParams(
            collective_id=0, has_side_effects=True, vmem_limit_bytes=63 * 1024 * 1024
        ),
    )(*operands)


def solution(mesh):
    def local(
        features,
        cotangent,
        first_gain,
        window_qkv,
        window_proj,
        window_table,
        second_gain,
        cross_qkv,
        cross_proj,
        cross_table,
    ):
        return body(
            mesh.shape["lat"],
            mesh.shape["lon"],
            features,
            cotangent,
            first_gain.reshape(1, CHANNELS),
            window_qkv,
            window_proj,
            window_table,
            second_gain.reshape(1, CHANNELS),
            cross_qkv,
            cross_proj,
            cross_table,
        )

    return jax.shard_map(
        local,
        mesh=mesh,
        in_specs=(
            P("lat", "lon", None),
            P("lat", "lon", None),
            P(),
            P(),
            P(),
            P(),
            P(),
            P(),
            P(),
            P(),
        ),
        out_specs=(P("lat", "lon", None), P(), P()),
        check_vma=False,
    )
```

time: 90.7 us -> 77.9 us (0.86)
  Pallas kernels: 86.7 us -> 74 us
    pallas_call x1, Pallas kernels: 86.7 us -> 74 us  [body(): pl.pallas_call(functools.partial(kernel, n_lat, n_lon), out_shape=(jax.Sh...]
where the time goes in v1:
time: 77.9 us; the launch traced here: 77.7 us
  Pallas kernels  74 us (95%)
  local copies, waits for them, and re-layouts  3.11 us (4%)
    pallas_call x1, Pallas kernels, body(): pl.pallas_call(functools.partial(kernel, n_lat, n_lon), out_shape=(jax.Sh...  74 us
    unnamed x7, local copies, waits for them, and re-layouts  3.11 us

profile of v1, /device:TPU:1, one launch (start us, length us, event | category | flops | bytes accessed | tf_op | source)
XLA Modules:
  0.0 77.7 jit_solution(13690199059119803962)
XLA Ops:
  0.6 74.0 %shard_map.121 = (f32[16,16,180]{2,1,0:T(8,128)}, f32[6,961]{1,0:T(8,128)}, f32[6,1521]{1,0:T(8,128)}) custom-call(bf16[16,16,180]{2,1,0:T(8,128)(2,1)} %feat_in.1, bf16[16,16,180]{2,1,0:T(8,128)(2,1)} %cot_in_hbm.1, f32[1,180]{1,0:T(1,128)} %bitcast.2, bf16[180,540]{1,0:T(8,128)(2,1)} %qkv1_in.1, bf16[180,180]{1,0:T(8,128)(2,1)} %proj1_in.1, ...), custom_call_target="tpu_custom_call" | custom-call | tf_op jit(solution)/shard_map/pallas_call | solution.py:947
  74.6 0.0 copy-start.1
  74.6 1.7 %copy.16 = f32[16,16,180]{2,1,0:T(8,128)} copy(f32[16,16,180]{2,1,0:T(8,128)} %get-tuple-element.6) | data formatting | bytes 368640
  76.3 0.0 copy-done.1
  76.3 0.0 copy-start
  76.3 0.6 copy.17
  76.9 0.2 copy-done
  77.1 0.6 copy.18
Async XLA Ops:
  74.6 1.7 %copy-start.1 = (f32[6,961]{1,0:T(8,128)S(1)}, f32[6,961]{1,0:T(8,128)}, u32[]{:S(2)}) copy-start(f32[6,961]{1,0:T(8,128)} %get-tuple-element.7) | copy-start | bytes 69196
  76.3 0.8 %copy-start = (f32[6,1521]{1,0:T(8,128)S(1)}, f32[6,1521]{1,0:T(8,128)}, u32[]{:S(2)}) copy-start(f32[6,1521]{1,0:T(8,128)} %get-tuple-element.8) | copy-start | bytes 109516

commit v2 on v1

--- a/solution.py
+++ b/solution.py
@@ -68,10 +68,6 @@
     return inverse * (scaled - first - unit * second)
 
 
-def slot(a, b):
-    return (a // 2 * 2 + b // 2) * 4 + a % 2 * 2 + b % 2
-
-
 OWN = [(sy, sx, 2 * sy + sx, (1 - sy) * 2 + (1 - sx)) for sy in (0, 1) for sx in (0, 1)]
 
 
@@ -109,6 +105,9 @@
     qkv2_in,
     proj2_in,
     tab2_in,
+    out_hbm,
+    out1_hbm,
+    out2_hbm,
     out_ref,
     out1_ref,
     out2_ref,
@@ -223,13 +222,12 @@
     def greet(dy, dx):
         pl.semaphore_signal(barrier, inc=1, device_id=at(dy, dx), device_id_type=MESH)
 
-    for dy in (-1, 1):
-        for dx in (-1, 1):
-            greet(dy, dx)
-    for j in range(1, n_lat):
+    for dy in (-1, 0, 1):
+        for dx in (-1, 0, 1):
+            if dy or dx:
+                greet(dy, dx)
+    for j in range(2, n_lat - 1):
         greet(j, 0)
-    greet(0, 1)
-    greet(0, -1)
     inner, outer = lon_plan(n_lon)
     spot = lax.rem(lon, inner)
 
@@ -248,7 +246,7 @@
     own = feat_ref[...].astype(F32)
     for sy, sx, w, s in OWN:
         quarter = own[8 * sy : 8 * sy + 8, 8 * sx : 8 * sx + 8, :].reshape(64, CHANNELS)
-        region[w * 4 + s] = quarter.astype(BF16)
+        region[1 + sy, 1 + sx] = quarter.astype(BF16)
 
     for load in loads[1:7]:
         load.wait()
@@ -272,27 +270,26 @@
 
     lax.fori_loop(0, 3, pad_weights, 0)
 
-    pl.semaphore_wait(barrier, 4 + 2 + n_lat - 1 + inner - 1 + outer - 1)
-
-    halo = []
-    for a in (1, 2):
-        for b in (1, 2):
-            for dy in (0, -1 if a == 1 else 1):
-                for dx in (0, -1 if b == 1 else 1):
-                    if dy == 0 and dx == 0:
-                        continue
-                    halo.append(
-                        pltpu.make_async_remote_copy(
-                            src_ref=region.at[slot(a, b)],
-                            dst_ref=region.at[slot(a - 2 * dy, b - 2 * dx)],
-                            send_sem=halo_send,
-                            recv_sem=halo_recv,
-                            device_id=at(dy, dx),
-                            device_id_type=MESH,
-                        )
-                    )
-    for copy in halo:
-        copy.start()
+    pl.semaphore_wait(barrier, 8 + n_lat - 3 + inner - 1 + outer - 1)
+
+    def side(step):
+        here = {-1: 1, 0: pl.ds(1, 2), 1: 2}[step]
+        there = {-1: 3, 0: pl.ds(1, 2), 1: 0}[step]
+        return here, there
+
+    for dy in (-1, 0, 1):
+        for dx in (-1, 0, 1):
+            if dy == 0 and dx == 0:
+                continue
+            (a, a_there), (b, b_there) = side(dy), side(dx)
+            pltpu.make_async_remote_copy(
+                src_ref=region.at[a, b],
+                dst_ref=region.at[a_there, b_there],
+                send_sem=halo_send,
+                recv_sem=halo_recv,
+                device_id=at(dy, dx),
+                device_id_type=MESH,
+            ).start()
 
     for load in loads[7:]:
         load.wait()
@@ -419,7 +416,7 @@
             into[rows, half : half + 128] = own_lanes
             into[rows, 128 - half : 256 - half] = zeros
 
-    every = region.at[pl.ds(0, 12)]
+    every = region.at[pl.ds(0, 3)]
     pltpu.make_async_copy(every, every, halo_recv).wait()
 
     gain1 = gain1_ref[...]
@@ -441,7 +438,7 @@
             w = 2 * wy + wx
             for c in range(4):
                 parts = [
-                    region[w * 4 + s, 16 * c : 16 * c + 16, :]
+                    region[2 * wy + s // 2, 2 * wx + s % 2, 16 * c : 16 * c + 16, :]
                     .astype(F32)
                     .reshape(2, 1, 8, CHANNELS)
                     for s in range(4)
@@ -754,7 +751,6 @@
     total = jnp.concatenate([total[0:4], total[4:12] + below[0:8], below[8:12]], axis=0)
     pair = [total[8 * sy : 8 * sy + 8].reshape(8, 1, 16, CHANNELS) for sy in range(2)]
     grad_mid[...] = jnp.concatenate(pair, axis=1).reshape(CELLS, CHANNELS)
-    sum_spread(0, tiles2, rs2, ag2)
 
     grads_t = dot_nt(pp1[...], grad_mid[...].astype(BF16))
     for h in range(HEADS):
@@ -776,7 +772,6 @@
                 return (ky % 8 * 4 + ky // 8 * 2 + sx) * 8
 
             collect(acc1, h, sx, 16, group_of, s1.at[0, h])
-    sum_cross(0, tiles2, ag2, far2)
 
     for h in range(HEADS):
         total = None
@@ -791,7 +786,7 @@
     for t in range(TILES_W):
         tiles1[t] = dense1[:HEADS, 128 * t : 128 * t + 128]
     sum_scatter(4, tiles1, rs1)
-    sum_gather(0, tiles2, far2, fin2)
+    sum_spread(0, tiles2, rs2, ag2)
 
     for h in range(HEADS):
         ot[0, own_rows(h), :] = dot(kt[own_rows(h), :], ds1[:, own_columns(h)])
@@ -799,6 +794,8 @@
     grad_queries = (jnp.transpose(ot[0]) * SCALE).astype(BF16)
     grad_keys = (dot(ds1[...], qm[...]) * SCALE).astype(BF16)
     grad_values = dot(p1[1], dom[...])
+    sum_spread(4, tiles1, rs1, ag1)
+    sum_cross(0, tiles2, ag2, far2)
     grad_first[...] = (
         dot(grad_queries, wt1[0:WIDE, :])
         + dot(grad_keys, wt1[WIDE : 2 * WIDE, :])
@@ -822,20 +819,29 @@
             device_id=at(s // 2, s % 2),
             device_id_type=MESH,
         ).start()
-    sum_spread(4, tiles1, rs1, ag1)
+    sum_cross(4, tiles1, ag1, far1)
+    sum_gather(0, tiles2, far2, fin2)
     drain(back_recv, back_in)
     out_ref[8:16, 0:8, :] = back_in[0].astype(F32).reshape(8, 8, CHANNELS)
     out_ref[0:8, 8:16, :] = back_in[1].astype(F32).reshape(8, 8, CHANNELS)
     out_ref[0:8, 0:8, :] = back_in[2].astype(F32).reshape(8, 8, CHANNELS)
-    sum_cross(4, tiles1, ag1, far1)
+    store = pltpu.make_async_copy(out_ref, out_hbm, load_sem.at[0])
+    store.start()
     sum_gather(4, tiles1, far1, fin1)
     sum_end(0, tiles2, rs2, ag2, far2, fin2)
     out2_ref[...] = joined(fin2, CROSS * CROSS)
+    store2 = pltpu.make_async_copy(out2_ref, out2_hbm, load_sem.at[1])
+    store2.start()
     sum_end(4, tiles1, rs1, ag1, far1, fin1)
+    out1_ref[...] = joined(fin1, SPAN * SPAN)
+    store1 = pltpu.make_async_copy(out1_ref, out1_hbm, load_sem.at[2])
+    store1.start()
     pltpu.make_async_copy(every, every, halo_send).wait()
     drain(mid_send, mid_out)
     drain(back_send, back_out)
-    out1_ref[...] = joined(fin1, SPAN * SPAN)
+    store.wait()
+    store2.wait()
+    store1.wait()
 
 
 def lon_plan(n_lon):
@@ -867,6 +873,9 @@
     tiles1, rs1, ag1, far1, fin1 = sums(TILES_W)
     tiles2, rs2, ag2, far2, fin2 = sums(TILES_C)
     scratch = [
+        vmem((16, 16, CHANNELS), F32),
+        vmem((HEADS, SPAN * SPAN), F32),
+        vmem((HEADS, CROSS * CROSS), F32),
         vmem((16, 16, CHANNELS), BF16),
         vmem((16, 16, CHANNELS), BF16),
         vmem((1, CHANNELS), F32),
@@ -878,7 +887,7 @@
         vmem((CHANNELS, CHANNELS), BF16),
         vmem((HEADS, CROSS * CROSS), F32),
         pltpu.SemaphoreType.DMA((10,)),
-        vmem((16, 64, CHANNELS), BF16),
+        vmem((4, 4, 64, CHANNELS), BF16),
         vmem((HEADS, LANES_W), F32),
         vmem((3, HEADS, LANES_C), F32),
         vmem((3 * WIDE, CHANNELS), BF16),
@@ -943,21 +952,42 @@
         pltpu.SemaphoreType.DMA((8,)),
         pltpu.SemaphoreType.DMA((8,)),
     ]
-    whole = pl.BlockSpec(memory_space=pltpu.VMEM)
-    return pl.pallas_call(
+    hbm = pl.BlockSpec(memory_space=pltpu.HBM)
+    limit = 63 * 1024 * 1024
+    shapes = (
+        jax.ShapeDtypeStruct((16, 16, CHANNELS), F32),
+        jax.ShapeDtypeStruct((HEADS, SPAN * SPAN), F32),
+        jax.ShapeDtypeStruct((HEADS, CROSS * CROSS), F32),
+    )
+    results = pl.pallas_call(
         functools.partial(kernel, n_lat, n_lon),
-        out_shape=(
-            jax.ShapeDtypeStruct((16, 16, CHANNELS), F32),
-            jax.ShapeDtypeStruct((HEADS, SPAN * SPAN), F32),
-            jax.ShapeDtypeStruct((HEADS, CROSS * CROSS), F32),
-        ),
-        in_specs=[pl.BlockSpec(memory_space=pltpu.HBM)] * 10,
-        out_specs=(whole, whole, whole),
+        out_shape=shapes,
+        in_specs=[hbm] * 10,
+        out_specs=(hbm,) * 3,
         scratch_shapes=scratch,
         compiler_params=pltpu.CompilerParams(
-            collective_id=0, has_side_effects=True, vmem_limit_bytes=63 * 1024 * 1024
+            collective_id=0, has_side_effects=True, vmem_limit_bytes=limit
         ),
     )(*operands)
+    return pl.pallas_call(
+        hand_over,
+        out_shape=shapes,
+        in_specs=[hbm] * 3,
+        out_specs=(hbm,) * 3,
+        scratch_shapes=[pltpu.SemaphoreType.DMA((3,))],
+        compiler_params=pltpu.CompilerParams(vmem_limit_bytes=limit),
+    )(*results)
+
+
+def hand_over(a, b, c, a_out, b_out, c_out, sems):
+    copies = [
+        pltpu.make_async_copy(src, dst, sems.at[i])
+        for i, (src, dst) in enumerate(((a, a_out), (b, b_out), (c, c_out)))
+    ]
+    for copy in copies:
+        copy.start()
+    for copy in copies:
+        copy.wait()
 
 
 def solution(mesh):

time: 77.9 us -> 76.1 us (0.977)
  local copies, waits for them, and re-layouts: 3.11 us -> 0 us
  Pallas kernels: 74 us -> 75.3 us
    unnamed x7 -> x0, local copies, waits for them, and re-layouts: 3.11 us -> none
    pallas_call x1 -> x2, Pallas kernels: 74 us -> 75.3 us  [the longest x1 63.8 us: body(): pl.pallas_call(functools.partial(kernel, n_lat, n_lon), out_shape=shapes,...]
where the time goes in v2:
time: 76.1 us; the launch traced here: 76 us
  Pallas kernels  75.3 us (99%)
    pallas_call x1, Pallas kernels, body(): pl.pallas_call(functools.partial(kernel, n_lat, n_lon), out_shape=shapes,...  63.8 us
    pallas_call x1, Pallas kernels, body(): pl.pallas_call(hand_over, out_shape=shapes, in_specs=[hbm] * 3, out_specs...  11.6 us

profile of v2, /device:TPU:1, one launch (start us, length us, event | category | flops | bytes accessed | tf_op | source)
XLA Modules:
  0.0 76.0 jit_solution(10077404712665014422)
XLA Ops:
  0.6 63.8 %shard_map.121 = (f32[16,16,180]{2,1,0:T(8,128)}, f32[6,961]{1,0:T(8,128)}, f32[6,1521]{1,0:T(8,128)}) custom-call(bf16[16,16,180]{2,1,0:T(8,128)(2,1)} %feat_in.1, bf16[16,16,180]{2,1,0:T(8,128)(2,1)} %cot_in_hbm.1, f32[1,180]{1,0:T(1,128)} %bitcast.2, bf16[180,540]{1,0:T(8,128)(2,1)} %qkv1_in.1, bf16[180,180]{1,0:T(8,128)(2,1)} %proj1_in.1, ...), custom_call_target="tpu_custom_call" | custom-call | tf_op jit(solution)/shard_map/pallas_call | solution.py:962
  64.4 11.6 %shard_map.122 = (f32[16,16,180]{2,1,0:T(8,128)}, f32[6,961]{1,0:T(8,128)}, f32[6,1521]{1,0:T(8,128)}) custom-call(f32[16,16,180]{2,1,0:T(8,128)} %get-tuple-element.6.a, f32[6,961]{1,0:T(8,128)} %get-tuple-element.7.b, f32[6,1521]{1,0:T(8,128)} %get-tuple-element.8.c), custom_call_target="tpu_custom_call" | custom-call | tf_op jit(solution)/shard_map/pallas_call | solution.py:972

commit v3 on v2

--- a/solution.py
+++ b/solution.py
@@ -246,7 +246,7 @@
     own = feat_ref[...].astype(F32)
     for sy, sx, w, s in OWN:
         quarter = own[8 * sy : 8 * sy + 8, 8 * sx : 8 * sx + 8, :].reshape(64, CHANNELS)
-        region[1 + sy, 1 + sx] = quarter.astype(BF16)
+        region[1 + sy, 1 + sx, :, :CHANNELS] = quarter.astype(BF16)
 
     for load in loads[1:7]:
         load.wait()
@@ -438,7 +438,7 @@
             w = 2 * wy + wx
             for c in range(4):
                 parts = [
-                    region[2 * wy + s // 2, 2 * wx + s % 2, 16 * c : 16 * c + 16, :]
+                    region[2 * wy + s // 2, 2 * wx + s % 2, 16 * c : 16 * c + 16, :CHANNELS]
                     .astype(F32)
                     .reshape(2, 1, 8, CHANNELS)
                     for s in range(4)
@@ -603,7 +603,7 @@
     for w in range(3):
         rows, cols = 12 * (w // 2), 16 * (w % 2)
         piece = lin[rows : rows + 12, cols : cols + 16, :]
-        mid_out[w] = piece.reshape(192, CHANNELS).astype(BF16)
+        mid_out[w, :, :CHANNELS] = piece.reshape(192, CHANNELS).astype(BF16)
         pltpu.make_async_remote_copy(
             src_ref=mid_out.at[w],
             dst_ref=mid_in.at[w],
@@ -711,12 +711,11 @@
             drain(sum_recv.at[kind + 3], result)
             drain(sum_send.at[kind], result)
 
-    def joined(result, count):
+    def joined(result):
         chunks, depth = result.shape[0], result.shape[1]
-        whole = jnp.concatenate(
+        return jnp.concatenate(
             [result[c, d] for c in range(chunks) for d in range(depth)], axis=1
         )
-        return whole[:, :count]
 
     def widened(part, width):
         return jnp.concatenate([part, jnp.zeros((8, width - part.shape[1]), F32)], axis=1)
@@ -738,7 +737,7 @@
     for t in range(TILES_C):
         part = pl.ds(128 * t, 128)
         whole = dense2[0, :, part] + dense2[1, :, part] + dense2[2, :, part]
-        tiles2[t] = whole[:HEADS]
+        tiles2[t] = whole
     sum_scatter(0, tiles2, rs2)
 
     vv[...] = dot_nt(normed[1], wt1[2 * WIDE :, :]).astype(BF16)
@@ -746,8 +745,8 @@
     head_lanes(dot_nt(normed[1], wt1[0:WIDE, :]), qm)
 
     drain(mid_recv, mid_in)
-    total = lin[12:24, 16:32, :] + mid_in[2].astype(F32).reshape(12, 16, CHANNELS)
-    below = (mid_in[0].astype(F32) + mid_in[1].astype(F32)).reshape(12, 16, CHANNELS)
+    total = lin[12:24, 16:32, :] + mid_in[2, :, :CHANNELS].astype(F32).reshape(12, 16, CHANNELS)
+    below = (mid_in[0, :, :CHANNELS].astype(F32) + mid_in[1, :, :CHANNELS].astype(F32)).reshape(12, 16, CHANNELS)
     total = jnp.concatenate([total[0:4], total[4:12] + below[0:8], below[8:12]], axis=0)
     pair = [total[8 * sy : 8 * sy + 8].reshape(8, 1, 16, CHANNELS) for sy in range(2)]
     grad_mid[...] = jnp.concatenate(pair, axis=1).reshape(CELLS, CHANNELS)
@@ -784,7 +783,7 @@
     for dy in range(SPAN):
         dense1[0:HEADS, dy * SPAN : (dy + 1) * SPAN] = flat1[:, dy * 32 : dy * 32 + SPAN]
     for t in range(TILES_W):
-        tiles1[t] = dense1[:HEADS, 128 * t : 128 * t + 128]
+        tiles1[t] = dense1[:, 128 * t : 128 * t + 128]
     sum_scatter(4, tiles1, rs1)
     sum_spread(0, tiles2, rs2, ag2)
 
@@ -806,10 +805,10 @@
         unit, inverse = norm_parts(feats[1, rows, :])
         grad = grad_mid[rows, :] + norm_back(unit, inverse, gain1, grad_first[rows, :])
         quarters = grad.reshape(2, 2, 2, 8, CHANNELS)
-        out_ref[8 + 2 * c : 10 + 2 * c, 8:16, :] = quarters[:, 0, 0]
+        out_ref[8 + 2 * c : 10 + 2 * c, 8:16, :CHANNELS] = quarters[:, 0, 0]
         for s in (1, 2, 3):
             piece = quarters[:, s // 2, s % 2].reshape(16, CHANNELS)
-            back_out[s - 1, 16 * c : 16 * c + 16, :] = piece.astype(BF16)
+            back_out[s - 1, 16 * c : 16 * c + 16, :CHANNELS] = piece.astype(BF16)
     for s in (1, 2, 3):
         pltpu.make_async_remote_copy(
             src_ref=back_out.at[s - 1],
@@ -822,18 +821,18 @@
     sum_cross(4, tiles1, ag1, far1)
     sum_gather(0, tiles2, far2, fin2)
     drain(back_recv, back_in)
-    out_ref[8:16, 0:8, :] = back_in[0].astype(F32).reshape(8, 8, CHANNELS)
-    out_ref[0:8, 8:16, :] = back_in[1].astype(F32).reshape(8, 8, CHANNELS)
-    out_ref[0:8, 0:8, :] = back_in[2].astype(F32).reshape(8, 8, CHANNELS)
+    out_ref[8:16, 0:8, :CHANNELS] = back_in[0, :, :CHANNELS].astype(F32).reshape(8, 8, CHANNELS)
+    out_ref[0:8, 8:16, :CHANNELS] = back_in[1, :, :CHANNELS].astype(F32).reshape(8, 8, CHANNELS)
+    out_ref[0:8, 0:8, :CHANNELS] = back_in[2, :, :CHANNELS].astype(F32).reshape(8, 8, CHANNELS)
     store = pltpu.make_async_copy(out_ref, out_hbm, load_sem.at[0])
     store.start()
     sum_gather(4, tiles1, far1, fin1)
     sum_end(0, tiles2, rs2, ag2, far2, fin2)
-    out2_ref[...] = joined(fin2, CROSS * CROSS)
+    out2_ref[...] = joined(fin2)
     store2 = pltpu.make_async_copy(out2_ref, out2_hbm, load_sem.at[1])
     store2.start()
     sum_end(4, tiles1, rs1, ag1, far1, fin1)
-    out1_ref[...] = joined(fin1, SPAN * SPAN)
+    out1_ref[...] = joined(fin1)
     store1 = pltpu.make_async_copy(out1_ref, out1_hbm, load_sem.at[2])
     store1.start()
     pltpu.make_async_copy(every, every, halo_send).wait()
@@ -863,19 +862,19 @@
         chunks = min(n_lat, count)
         depth = count // chunks
         return (
-            vmem((count, HEADS, 128), F32),
-            vmem((n_lat - 1, depth, HEADS, 128), F32),
-            vmem((inner, depth, HEADS, 128), F32),
-            vmem((outer, depth, HEADS, 128), F32),
-            vmem((chunks, depth, HEADS, 128), F32),
+            vmem((count, 8, 128), F32),
+            vmem((n_lat - 1, depth, 8, 128), F32),
+            vmem((inner, depth, 8, 128), F32),
+            vmem((outer, depth, 8, 128), F32),
+            vmem((chunks, depth, 8, 128), F32),
         )
 
     tiles1, rs1, ag1, far1, fin1 = sums(TILES_W)
     tiles2, rs2, ag2, far2, fin2 = sums(TILES_C)
     scratch = [
-        vmem((16, 16, CHANNELS), F32),
-        vmem((HEADS, SPAN * SPAN), F32),
-        vmem((HEADS, CROSS * CROSS), F32),
+        vmem((16, 16, WIDE), F32),
+        vmem((8, 128 * TILES_W), F32),
+        vmem((8, 128 * TILES_C), F32),
         vmem((16, 16, CHANNELS), BF16),
         vmem((16, 16, CHANNELS), BF16),
         vmem((1, CHANNELS), F32),
@@ -887,7 +886,7 @@
         vmem((CHANNELS, CHANNELS), BF16),
         vmem((HEADS, CROSS * CROSS), F32),
         pltpu.SemaphoreType.DMA((10,)),
-        vmem((4, 4, 64, CHANNELS), BF16),
+        vmem((4, 4, 64, WIDE), BF16),
         vmem((HEADS, LANES_W), F32),
         vmem((3, HEADS, LANES_C), F32),
         vmem((3 * WIDE, CHANNELS), BF16),
@@ -927,10 +926,10 @@
         vmem((KEYS, WIDE), BF16),
         vmem((WIDE, KEYS), BF16),
         vmem((KEY_SIDE, 32, CHANNELS), F32),
-        vmem((3, 192, CHANNELS), BF16),
-        vmem((3, 192, CHANNELS), BF16),
-        vmem((3, 64, CHANNELS), BF16),
-        vmem((3, 64, CHANNELS), BF16),
+        vmem((3, 192, WIDE), BF16),
+        vmem((3, 192, WIDE), BF16),
+        vmem((3, 64, WIDE), BF16),
+        vmem((3, 64, WIDE), BF16),
         vmem((8, 128 * TILES_W), F32),
         vmem((3, 8, 128 * TILES_C), F32),
         tiles1,
@@ -955,11 +954,11 @@
     hbm = pl.BlockSpec(memory_space=pltpu.HBM)
     limit = 63 * 1024 * 1024
     shapes = (
-        jax.ShapeDtypeStruct((16, 16, CHANNELS), F32),
-        jax.ShapeDtypeStruct((HEADS, SPAN * SPAN), F32),
-        jax.ShapeDtypeStruct((HEADS, CROSS * CROSS), F32),
+        jax.ShapeDtypeStruct((16, 16, WIDE), F32),
+        jax.ShapeDtypeStruct((8, 128 * TILES_W), F32),
+        jax.ShapeDtypeStruct((8, 128 * TILES_C), F32),
     )
-    results = pl.pallas_call(
+    grads, grad1, grad2 = pl.pallas_call(
         functools.partial(kernel, n_lat, n_lon),
         out_shape=shapes,
         in_specs=[hbm] * 10,
@@ -969,25 +968,11 @@
             collective_id=0, has_side_effects=True, vmem_limit_bytes=limit
         ),
     )(*operands)
-    return pl.pallas_call(
-        hand_over,
-        out_shape=shapes,
-        in_specs=[hbm] * 3,
-        out_specs=(hbm,) * 3,
-        scratch_shapes=[pltpu.SemaphoreType.DMA((3,))],
-        compiler_params=pltpu.CompilerParams(vmem_limit_bytes=limit),
-    )(*results)
-
-
-def hand_over(a, b, c, a_out, b_out, c_out, sems):
-    copies = [
-        pltpu.make_async_copy(src, dst, sems.at[i])
-        for i, (src, dst) in enumerate(((a, a_out), (b, b_out), (c, c_out)))
-    ]
-    for copy in copies:
-        copy.start()
-    for copy in copies:
-        copy.wait()
+    return (
+        grads[:, :, :CHANNELS],
+        grad1[:HEADS, : SPAN * SPAN],
+        grad2[:HEADS, : CROSS * CROSS],
+    )
 
 
 def solution(mesh):

time: 76.1 us -> 67.9 us (0.89)
  Pallas kernels: 75.3 us -> 63.9 us
  local copies, waits for them, and re-layouts: 0 us -> 3.11 us
    pallas_call x1 -> x0, Pallas kernels: 11.6 us -> none  [body(): pl.pallas_call(hand_over, out_shape=shapes, in_specs=[hbm] * 3, out_specs...]
    unnamed x0 -> x7, local copies, waits for them, and re-layouts: none -> 3.11 us
where the time goes in v3:
time: 67.9 us; the launch traced here: 67.7 us
  Pallas kernels  63.9 us (94%)
  local copies, waits for them, and re-layouts  3.11 us (5%)
    pallas_call x1, Pallas kernels, body(): pl.pallas_call(functools.partial(kernel, n_lat, n_lon), out_shape=shapes,...  63.9 us
    unnamed x7, local copies, waits for them, and re-layouts  3.11 us

profile of v3, /device:TPU:1, one launch (start us, length us, event | category | flops | bytes accessed | tf_op | source)
XLA Modules:
  0.0 67.7 jit_solution(12058944281911977711)
XLA Ops:
  0.6 63.9 %shard_map.121 = (f32[16,16,256]{2,1,0:T(8,128)}, f32[8,1024]{1,0:T(8,128)}, f32[8,1536]{1,0:T(8,128)}) custom-call(bf16[16,16,180]{2,1,0:T(8,128)(2,1)} %feat_in.1, bf16[16,16,180]{2,1,0:T(8,128)(2,1)} %cot_in_hbm.1, f32[1,180]{1,0:T(1,128)} %bitcast.8, bf16[180,540]{1,0:T(8,128)(2,1)} %qkv1_in.1, bf16[180,180]{1,0:T(8,128)(2,1)} %proj1_in.1, ...), custom_call_target="tpu_custom_call" | custom-call | tf_op jit(solution)/shard_map/pallas_call | solution.py:961
  64.5 0.0 copy-start.1
  64.5 1.7 %copy.16 = f32[16,16,180]{2,1,0:T(8,128)} copy(f32[16,16,180]{2,1,0:T(8,128)} %bitcast.5) | data formatting | bytes 368640
  66.2 0.0 copy-done.1
  66.2 0.0 copy-start
  66.2 0.6 copy.17
  66.8 0.2 copy-done
  67.0 0.6 copy.18
Async XLA Ops:
  64.5 1.7 %copy-start.1 = (f32[8,1024]{1,0:T(8,128)S(1)}, f32[8,1024]{1,0:T(8,128)}, u32[]{:S(2)}) copy-start(f32[8,1024]{1,0:T(8,128)} %get-tuple-element.7) | copy-start | bytes 98308
  66.2 0.8 %copy-start = (f32[8,1536]{1,0:T(8,128)S(1)}, f32[8,1536]{1,0:T(8,128)}, u32[]{:S(2)}) copy-start(f32[8,1536]{1,0:T(8,128)} %get-tuple-element.8) | copy-start | bytes 147460

commit v4 on v3

--- a/solution.py
+++ b/solution.py
@@ -309,9 +309,9 @@
         for s in range(3):
             start = dy * CROSS + 8 * s
             flat2[s, :, dy * 32 : dy * 32 + 23] = tab2_ref[:, start : start + 23]
-    def spread(pair, _):
-        for i in range(2):
-            h = 2 * pair + i
+    def spread(group, _):
+        for i in range(3):
+            h = 3 * group + i
             row = pl.ds(h, 1)
             for s in range(2):
                 base = jnp.broadcast_to(flat1[row, :] * LOG2E, (8, LANES_W))
@@ -323,7 +323,7 @@
                     z2[s, r, h] = part[:, :USED_C]
         return 0
 
-    lax.fori_loop(0, HEADS // 2, spread, 0)
+    lax.fori_loop(0, HEADS // 3, spread, 0)
     query_half = (iota((1, CELLS), 1) >> 4) & 1
 
     def window_bias(h, y8):
@@ -402,10 +402,6 @@
             pieces.append(jnp.zeros((128 - HEAD_PAD - before, CELLS), rows.dtype))
         return jnp.concatenate(pieces, axis=0) if len(pieces) > 1 else rows
 
-    def head_block(rows, h):
-        four = jnp.concatenate([rows] * 4, axis=0)
-        return jnp.where((iota((128, CELLS), 0) >> 5) == lax.rem(h, 4), four, 0.0).astype(BF16)
-
     def head_lanes(values, into):
         zeros = jnp.zeros((CELLS, 128), BF16)
         for h in range(HEADS):
@@ -433,55 +429,48 @@
     def own_rows(h):
         return slice(h * HEAD_PAD, (h + 1) * HEAD_PAD)
 
-    def window_row(wy, _):
-        for wx in range(2):
-            w = 2 * wy + wx
-            for c in range(4):
-                parts = [
-                    region[2 * wy + s // 2, 2 * wx + s % 2, 16 * c : 16 * c + 16, :CHANNELS]
-                    .astype(F32)
-                    .reshape(2, 1, 8, CHANNELS)
-                    for s in range(4)
-                ]
-                values = jnp.concatenate(parts, axis=1).reshape(64, CHANNELS)
-                rows = slice(64 * c, 64 * c + 64)
-                feats[wx, rows, :] = values
-                unit, _ = norm_parts(values)
-                normed[wx, rows, :] = (unit * gain1).astype(BF16)
-        edge = lat == jnp.where(wy == 0, 0, n_lat - 1)
-        floor = jnp.where(edge, NEGATIVE, 0.0)
-        hidden = jnp.where(pad_row - 30 == 1 - query_half, floor, 0.0)
-        hidden = jnp.where(pad_row >= 30, hidden, 0.0)
-        for wx in range(2):
-            queries = dot_nt(wt1[0:WIDE, :], normed[wx])
-            for h in range(HEADS):
-                qmt[wx, h] = head_rows((queries[own_rows(h), :] + hidden).astype(BF16), h)
-            keys = dot_nt(normed[wx], wt1[WIDE : 2 * WIDE, :])
-            kk[wx] = jnp.where(marks, 1.0, keys).astype(BF16)
-            vt[wx] = dot_nt(wt1[2 * WIDE :, :], normed[wx]).astype(BF16)
-        for wx in range(2):
-            for h in range(HEADS):
-                half = h // 4 * 128
-                s1[wx, h] = dot(kk[wx, :, half : half + 128], qmt[wx, h])
-        for wx in range(2):
-            for h in range(HEADS):
-                scores = s1.at[wx, h]
-                peak = add_bias(scores, 32, 8, functools.partial(window_bias, h))
-                inverse = raise_all(scores, 32, 8, peak, p1.at[wx], own_columns(h), False)
-                inverse1[wx, h] = inverse
-        for wx in range(2):
-            for h in range(HEADS):
-                rows = own_rows(h)
-                heads_t = dot(vt[wx, rows, :], p1[wx, :, own_columns(h)])
-                ot[wx, rows, :] = heads_t * inverse1[wx, h]
-        for wx in range(2):
-            heads_out = jnp.transpose(ot[wx]).astype(BF16)
-            middle = feats[wx] + dot(heads_out, pp1[...])
-            middles[2 * wy + wx] = middle.reshape(8, 2, 2, 8, CHANNELS)
-        return 0
-
-    ot[...] = jnp.zeros(ot.shape, F32)
-    lax.fori_loop(0, 2, window_row, 0)
+    for w in range(4):
+        for c in range(4):
+            parts = [
+                region[w // 2 * 2 + s // 2, w % 2 * 2 + s % 2, 16 * c : 16 * c + 16, :CHANNELS]
+                .astype(F32)
+                .reshape(2, 1, 8, CHANNELS)
+                for s in range(4)
+            ]
+            values = jnp.concatenate(parts, axis=1).reshape(64, CHANNELS)
+            rows = slice(64 * c, 64 * c + 64)
+            feats[w, rows, :] = values
+            unit, _ = norm_parts(values)
+            normed[w, rows, :] = (unit * gain1).astype(BF16)
+    for w in range(4):
+        if w % 2 == 0:
+            floor = jnp.where(lat == (0 if w == 0 else n_lat - 1), NEGATIVE, 0.0)
+            hidden = jnp.where(pad_row - 30 == 1 - query_half, floor, 0.0)
+            hidden = jnp.where(pad_row >= 30, hidden, 0.0)
+        queries = dot_nt(wt1[0:WIDE, :], normed[w])
+        for h in range(HEADS):
+            qmt[w, h] = head_rows((queries[own_rows(h), :] + hidden).astype(BF16), h)
+        keys = dot_nt(normed[w], wt1[WIDE : 2 * WIDE, :])
+        kk[w] = jnp.where(marks, 1.0, keys).astype(BF16)
+        vt[w] = dot_nt(wt1[2 * WIDE :, :], normed[w]).astype(BF16)
+    for w in range(4):
+        for h in range(HEADS):
+            half = h // 4 * 128
+            s1[w, h] = dot(kk[w, :, half : half + 128], qmt[w, h])
+    for w in range(4):
+        for h in range(HEADS):
+            scores = s1.at[w, h]
+            peak = add_bias(scores, 32, 8, functools.partial(window_bias, h))
+            inverse1[w, h] = raise_all(scores, 32, 8, peak, p1.at[w], own_columns(h), False)
+    for w in range(4):
+        for h in range(HEADS):
+            heads_t = dot(vt[w, own_rows(h), :], p1[w, :, own_columns(h)])
+            ot[w, own_rows(h), :] = heads_t * inverse1[w, h]
+        ot[w, HEADS * HEAD_PAD :, :] = jnp.zeros((WIDE - HEADS * HEAD_PAD, CELLS), F32)
+    for w in range(4):
+        heads_out = jnp.transpose(ot[w]).astype(BF16)
+        middle = feats[w] + dot(heads_out, pp1[...])
+        middles[w] = middle.reshape(8, 2, 2, 8, CHANNELS)
 
     y_runs = ((0, 0, 4, 8, 0), (0, 1, 0, 8, 4), (1, 0, 0, 8, 12), (1, 1, 0, 4, 20))
     for wy, sy, first, last, place in y_runs:
@@ -492,18 +481,13 @@
                     2 * wy + wx, first:last, sy, sx
                 ]
 
-    def second_norm(step, _):
-        for k in range(4):
-            i = 4 * step + k
-            lines, rows = pl.ds(2 * i, 2), pl.ds(pl.multiple_of(64 * i, 64), 64)
-            unit, inverse = norm_parts(lin[lines].reshape(64, CHANNELS))
-            units[rows, :] = unit
-            inverses[rows, :] = inverse
-            normal = (unit * gain2).astype(BF16).astype(F32)
-            lin[lines] = normal.reshape(2, 32, CHANNELS)
-        return 0
-
-    lax.fori_loop(0, KEY_SIDE // 8, second_norm, 0)
+    for i in range(KEY_SIDE // 2):
+        lines, rows = slice(2 * i, 2 * i + 2), slice(64 * i, 64 * i + 64)
+        unit, inverse = norm_parts(lin[lines].reshape(64, CHANNELS))
+        units[rows, :] = unit
+        inverses[rows, :] = inverse
+        normal = (unit * gain2).astype(BF16).astype(F32)
+        lin[lines] = normal.reshape(2, 32, CHANNELS)
     inside_low = jnp.where(lat > 0, 1.0, 0.0)
     inside_high = jnp.where(lat < n_lat - 1, 1.0, 0.0)
     lin[0:4] = lin[0:4] * inside_low
@@ -533,45 +517,31 @@
         qmt[0, h] = head_rows(queries_t[h * HEAD_PAD : (h + 1) * HEAD_PAD, :], h)
     head_lanes(dot_nt(queries_in, wt2[0:WIDE, :]), qm)
 
-    def cross_heads(group, _):
-        heads = [3 * group + i for i in range(3)]
-
-        def half(h):
-            return pl.ds(pl.multiple_of(h // 4 * 128, 128), 128)
-
-        def columns(h):
-            return pl.ds(pl.multiple_of(h * CELLS, CELLS), CELLS)
-
-        def rows(h):
-            return pl.ds(pl.multiple_of(h * HEAD_PAD, HEAD_PAD), HEAD_PAD)
-
-        def bias(h, c):
-            return jnp.concatenate([cross_bias(h, 2 * c), cross_bias(h, 2 * c + 1)], axis=0)
-
-        for i, h in enumerate(heads):
-            s2[i] = dot(k2[:, half(h)], qmt[0, h])
-        inverse = []
-        for i, h in enumerate(heads):
-            peak = add_bias(s2.at[i], 48, 12, functools.partial(bias, h))
-            inverse.append(raise_all(s2.at[i], 48, 12, peak, p2, columns(h), True))
-            scaled = gt[rows(h), :] * inverse[i]
-            gt[rows(h), :] = scaled
-            g2[i] = dot(v2[:, half(h)], head_block(scaled, h))
-        for i, h in enumerate(heads):
-            scores, grads = s2.at[i], g2.at[i]
-
-            def raised(part):
-                return scores[part, :]
-
-            total = weigh_all(raised, grads, 48, 12, inverse[i])
-            slope_all(raised, grads, 48, 12, total, scores, ds2, columns(h))
-            for s in range(3):
-                collect(acc2, h, s, KEY_SIDE, lambda m: (m * 3 + s) * 8, scores)
-        for h in heads:
-            ot[0, rows(h), :] = dot(k2t[rows(h), :], ds2[:, columns(h)])
-        return 0
-
-    lax.fori_loop(0, HEADS // 3, cross_heads, 0)
+    def bias(h, c):
+        return jnp.concatenate([cross_bias(h, 2 * c), cross_bias(h, 2 * c + 1)], axis=0)
+
+    for h in range(HEADS):
+        half = h // 4 * 128
+        s2[h] = dot(k2[:, half : half + 128], qmt[0, h])
+    inverse2 = []
+    for h in range(HEADS):
+        half = h // 4 * 128
+        peak = add_bias(s2.at[h], 48, 12, functools.partial(bias, h))
+        inverse2.append(raise_all(s2.at[h], 48, 12, peak, p2, own_columns(h), True))
+        scaled = gt[own_rows(h), :] * inverse2[h]
+        gt[own_rows(h), :] = scaled
+        g2[h] = dot(v2[:, half : half + 128], head_rows(scaled.astype(BF16), h))
+    for h in range(HEADS):
+
+        def raised(part):
+            return s2[h, part, :]
+
+        total = weigh_all(raised, g2.at[h], 48, 12, inverse2[h])
+        slope_all(raised, g2.at[h], 48, 12, total, s2.at[h], ds2, own_columns(h))
+        for s in range(3):
+            collect(acc2, h, s, KEY_SIDE, lambda m: (m * 3 + s) * 8, s2.at[h])
+    for h in range(HEADS):
+        ot[0, own_rows(h), :] = dot(k2t[own_rows(h), :], ds2[:, own_columns(h)])
     head_lanes(jnp.transpose(gt[...]), dom)
     grad_queries = (jnp.transpose(ot[0]) * SCALE).astype(BF16)
     grad_keys = (dot(ds2[...], qm[...]) * SCALE).astype(BF16)
@@ -587,16 +557,11 @@
         place = (*own_part(sy, sx), slice(None))
         lin[place] = lin[place] + grad_own[64 * i : 64 * i + 64, :].reshape(8, 8, CHANNELS)
 
-    def second_back(step, _):
-        for k in range(4):
-            i = 4 * step + k
-            lines, rows = pl.ds(2 * i, 2), pl.ds(pl.multiple_of(64 * i, 64), 64)
-            grad = lin[lines].reshape(64, CHANNELS)
-            grad = norm_back(units[rows, :], inverses[rows, :], gain2, grad)
-            lin[lines] = grad.reshape(2, 32, CHANNELS)
-        return 0
-
-    lax.fori_loop(0, KEY_SIDE // 8, second_back, 0)
+    for i in range(KEY_SIDE // 2):
+        lines, rows = slice(2 * i, 2 * i + 2), slice(64 * i, 64 * i + 64)
+        grad = lin[lines].reshape(64, CHANNELS)
+        grad = norm_back(units[rows, :], inverses[rows, :], gain2, grad)
+        lin[lines] = grad.reshape(2, 32, CHANNELS)
     for i, (sy, sx, w, s) in enumerate(OWN):
         place = (*own_part(sy, sx), slice(None))
         lin[place] = lin[place] + cot_own[i].reshape(8, 8, CHANNELS)
@@ -720,15 +685,15 @@
     def widened(part, width):
         return jnp.concatenate([part, jnp.zeros((8, width - part.shape[1]), F32)], axis=1)
 
-    def gather_cross(pair, _):
-        for i in range(2):
-            h = 2 * pair + i
+    def gather_cross(group, _):
+        for i in range(3):
+            h = 3 * group + i
             for s in range(3):
                 parts = [widened(acc2[s, r, h], LANES_C) for r in range(4)]
                 flat2[s, pl.ds(h, 1), :] = gather_rows(parts, -1)
         return 0
 
-    lax.fori_loop(0, HEADS // 2, gather_cross, 0)
+    lax.fori_loop(0, HEADS // 3, gather_cross, 0)
     dense2[...] = jnp.zeros(dense2.shape, F32)
     for dy in range(CROSS):
         for s in range(3):
@@ -740,9 +705,9 @@
         tiles2[t] = whole
     sum_scatter(0, tiles2, rs2)
 
-    vv[...] = dot_nt(normed[1], wt1[2 * WIDE :, :]).astype(BF16)
-    kt[...] = dot_nt(wt1[WIDE : 2 * WIDE, :], normed[1]).astype(BF16)
-    head_lanes(dot_nt(normed[1], wt1[0:WIDE, :]), qm)
+    vv[...] = dot_nt(normed[3], wt1[2 * WIDE :, :]).astype(BF16)
+    kt[...] = dot_nt(wt1[WIDE : 2 * WIDE, :], normed[3]).astype(BF16)
+    head_lanes(dot_nt(normed[3], wt1[0:WIDE, :]), qm)
 
     drain(mid_recv, mid_in)
     total = lin[12:24, 16:32, :] + mid_in[2, :, :CHANNELS].astype(F32).reshape(12, 16, CHANNELS)
@@ -753,16 +718,16 @@
 
     grads_t = dot_nt(pp1[...], grad_mid[...].astype(BF16))
     for h in range(HEADS):
-        scaled = grads_t[own_rows(h), :] * inverse1[1, h]
+        scaled = grads_t[own_rows(h), :] * inverse1[3, h]
         gt[own_rows(h), :] = scaled
         half = h // 4 * 128
         s1[1, h] = dot(vv[:, half : half + 128], head_rows(scaled.astype(BF16), h))
     for h in range(HEADS):
 
         def raised(part):
-            return p1[1, part, own_columns(h)].astype(F32)
-
-        total = weigh_all(raised, s1.at[1, h], 32, 8, inverse1[1, h])
+            return p1[3, part, own_columns(h)].astype(F32)
+
+        total = weigh_all(raised, s1.at[1, h], 32, 8, inverse1[3, h])
         slope_all(raised, s1.at[1, h], 32, 8, total, s1.at[0, h], ds1, own_columns(h))
         for sx in range(2):
 
@@ -792,7 +757,7 @@
     head_lanes(jnp.transpose(gt[...]), dom)
     grad_queries = (jnp.transpose(ot[0]) * SCALE).astype(BF16)
     grad_keys = (dot(ds1[...], qm[...]) * SCALE).astype(BF16)
-    grad_values = dot(p1[1], dom[...])
+    grad_values = dot(p1[3], dom[...])
     sum_spread(4, tiles1, rs1, ag1)
     sum_cross(0, tiles2, ag2, far2)
     grad_first[...] = (
@@ -802,7 +767,7 @@
     )
     for c in range(4):
         rows = slice(64 * c, 64 * c + 64)
-        unit, inverse = norm_parts(feats[1, rows, :])
+        unit, inverse = norm_parts(feats[3, rows, :])
         grad = grad_mid[rows, :] + norm_back(unit, inverse, gain1, grad_first[rows, :])
         quarters = grad.reshape(2, 2, 2, 8, CHANNELS)
         out_ref[8 + 2 * c : 10 + 2 * c, 8:16, :CHANNELS] = quarters[:, 0, 0]
@@ -898,27 +863,27 @@
         vmem((3, 4, HEADS, 8, USED_C), F32),
         vmem((2, 4, HEADS, 8, USED_W), F32),
         vmem((3, 4, HEADS, 8, USED_C), F32),
-        vmem((2, CELLS, CHANNELS), F32),
+        vmem((4, CELLS, CHANNELS), F32),
         vmem((4, 8, 2, 2, 8, CHANNELS), F32),
         vmem((KEY_SIDE * 32, CHANNELS), F32),
         vmem((KEY_SIDE * 32, 1), F32),
-        vmem((2, CELLS, WIDE), BF16),
-        vmem((2, WIDE, CELLS), BF16),
+        vmem((4, CELLS, WIDE), BF16),
+        vmem((4, WIDE, CELLS), BF16),
         vmem((CELLS, WIDE), BF16),
         vmem((WIDE, CELLS), BF16),
         vmem((HEADS * CELLS, WIDE), BF16),
         vmem((HEADS * CELLS, WIDE), BF16),
-        vmem((2, HEADS, 128, CELLS), BF16),
+        vmem((4, HEADS, 128, CELLS), BF16),
         vmem((WIDE, CELLS), F32),
-        vmem((2, WIDE, CELLS), F32),
-        vmem((2, CELLS, CHANNELS), BF16),
-        vmem((2, HEADS, 1, CELLS), F32),
-        vmem((2, HEADS, CELLS, CELLS), F32),
-        vmem((3, KEYS, CELLS), F32),
-        vmem((3, KEYS, CELLS), F32),
+        vmem((4, WIDE, CELLS), F32),
+        vmem((4, CELLS, CHANNELS), BF16),
+        vmem((4, HEADS, 1, CELLS), F32),
+        vmem((4, HEADS, CELLS, CELLS), F32),
+        vmem((HEADS, KEYS, CELLS), F32),
+        vmem((HEADS, KEYS, CELLS), F32),
         vmem((CELLS, CHANNELS), F32),
         vmem((CELLS, CHANNELS), F32),
-        vmem((2, CELLS, HEADS * CELLS), BF16),
+        vmem((4, CELLS, HEADS * CELLS), BF16),
         vmem((KEYS, HEADS * CELLS), BF16),
         vmem((CELLS, HEADS * CELLS), BF16),
         vmem((KEYS, HEADS * CELLS), BF16),

time: 67.9 us -> 65.2 us (0.960)
  Pallas kernels: 63.9 us -> 61.3 us
    pallas_call x1, Pallas kernels: 63.9 us -> 61.3 us  [body(): pl.pallas_call(functools.partial(kernel, n_lat, n_lon), out_shape=shapes,...]
where the time goes in v4:
time: 65.2 us; the launch traced here: 65 us
  Pallas kernels  61.3 us (94%)
  local copies, waits for them, and re-layouts  3.11 us (5%)
    pallas_call x1, Pallas kernels, body(): pl.pallas_call(functools.partial(kernel, n_lat, n_lon), out_shape=shapes,...  61.3 us
    unnamed x7, local copies, waits for them, and re-layouts  3.11 us

profile of v4, /device:TPU:1, one launch (start us, length us, event | category | flops | bytes accessed | tf_op | source)
XLA Modules:
  0.0 65.0 jit_solution(2619602220426891658)
XLA Ops:
  0.6 61.3 %shard_map.121 = (f32[16,16,256]{2,1,0:T(8,128)}, f32[8,1024]{1,0:T(8,128)}, f32[8,1536]{1,0:T(8,128)}) custom-call(bf16[16,16,180]{2,1,0:T(8,128)(2,1)} %feat_in.1, bf16[16,16,180]{2,1,0:T(8,128)(2,1)} %cot_in_hbm.1, f32[1,180]{1,0:T(1,128)} %bitcast.8, bf16[180,540]{1,0:T(8,128)(2,1)} %qkv1_in.1, bf16[180,180]{1,0:T(8,128)(2,1)} %proj1_in.1, ...), custom_call_target="tpu_custom_call" | custom-call | tf_op jit(solution)/shard_map/pallas_call | solution.py:926
  61.9 0.0 copy-start.1
  61.9 1.7 %copy.16 = f32[16,16,180]{2,1,0:T(8,128)} copy(f32[16,16,180]{2,1,0:T(8,128)} %bitcast.5) | data formatting | bytes 368640
  63.6 0.0 copy-done.1
  63.6 0.0 copy-start
  63.6 0.6 copy.17
  64.2 0.2 copy-done
  64.4 0.6 copy.18
Async XLA Ops:
  61.9 1.7 %copy-start.1 = (f32[8,1024]{1,0:T(8,128)S(1)}, f32[8,1024]{1,0:T(8,128)}, u32[]{:S(2)}) copy-start(f32[8,1024]{1,0:T(8,128)} %get-tuple-element.7) | copy-start | bytes 98308
  63.6 0.8 %copy-start = (f32[8,1536]{1,0:T(8,128)S(1)}, f32[8,1536]{1,0:T(8,128)}, u32[]{:S(2)}) copy-start(f32[8,1536]{1,0:T(8,128)} %get-tuple-element.8) | copy-start | bytes 147460

commit v5 on v4

--- a/solution.py
+++ b/solution.py
@@ -251,24 +251,17 @@
     for load in loads[1:7]:
         load.wait()
 
-    def pad_weights(i, _):
+    for i in range(3):
         lane = iota((WIDE, 1), 0)
         real = (lane < 192) & ((lane & 31) < HEAD_SIZE)
         source = jnp.where(real, CHANNELS * i + lane - 2 * (lane >> 5), -1)
         pick = one_hot(iota((WIDE, 3 * CHANNELS), 1) == source)
-        rows = pl.ds(pl.multiple_of(i * WIDE, WIDE), WIDE)
+        rows = slice(i * WIDE, (i + 1) * WIDE)
         wt1[rows, :] = dot_nt(pick, qkv1_ref[...]).astype(BF16)
         wt2[rows, :] = dot_nt(pick, qkv2_ref[...]).astype(BF16)
-
-        @pl.when(i == 0)
-        def _():
-            pick_proj = pick[:, :CHANNELS]
-            pp1[...] = dot(pick_proj, proj1_ref[...]).astype(BF16)
-            pp2[...] = dot(pick_proj, proj2_ref[...]).astype(BF16)
-
-        return 0
-
-    lax.fori_loop(0, 3, pad_weights, 0)
+        if i == 0:
+            pp1[...] = dot(pick[:, :CHANNELS], proj1_ref[...]).astype(BF16)
+            pp2[...] = dot(pick[:, :CHANNELS], proj2_ref[...]).astype(BF16)
 
     pl.semaphore_wait(barrier, 8 + n_lat - 3 + inner - 1 + outer - 1)
 
@@ -538,8 +531,6 @@
 
         total = weigh_all(raised, g2.at[h], 48, 12, inverse2[h])
         slope_all(raised, g2.at[h], 48, 12, total, s2.at[h], ds2, own_columns(h))
-        for s in range(3):
-            collect(acc2, h, s, KEY_SIDE, lambda m: (m * 3 + s) * 8, s2.at[h])
     for h in range(HEADS):
         ot[0, own_rows(h), :] = dot(k2t[own_rows(h), :], ds2[:, own_columns(h)])
     head_lanes(jnp.transpose(gt[...]), dom)
@@ -685,6 +676,10 @@
     def widened(part, width):
         return jnp.concatenate([part, jnp.zeros((8, width - part.shape[1]), F32)], axis=1)
 
+    for h in range(HEADS):
+        for s in range(3):
+            collect(acc2, h, s, KEY_SIDE, lambda m: (m * 3 + s) * 8, s2.at[h])
+
     def gather_cross(group, _):
         for i in range(3):
             h = 3 * group + i
@@ -706,9 +701,6 @@
     sum_scatter(0, tiles2, rs2)
 
     vv[...] = dot_nt(normed[3], wt1[2 * WIDE :, :]).astype(BF16)
-    kt[...] = dot_nt(wt1[WIDE : 2 * WIDE, :], normed[3]).astype(BF16)
-    head_lanes(dot_nt(normed[3], wt1[0:WIDE, :]), qm)
-
     drain(mid_recv, mid_in)
     total = lin[12:24, 16:32, :] + mid_in[2, :, :CHANNELS].astype(F32).reshape(12, 16, CHANNELS)
     below = (mid_in[0, :, :CHANNELS].astype(F32) + mid_in[1, :, :CHANNELS].astype(F32)).reshape(12, 16, CHANNELS)
@@ -751,6 +743,8 @@
         tiles1[t] = dense1[:, 128 * t : 128 * t + 128]
     sum_scatter(4, tiles1, rs1)
     sum_spread(0, tiles2, rs2, ag2)
+    kt[...] = dot_nt(wt1[WIDE : 2 * WIDE, :], normed[3]).astype(BF16)
+    head_lanes(dot_nt(normed[3], wt1[0:WIDE, :]), qm)
 
     for h in range(HEADS):
         ot[0, own_rows(h), :] = dot(kt[own_rows(h), :], ds1[:, own_columns(h)])

time: 65.2 us -> 65.7 us (level)
  no operation moved by 1% of the time
where the time goes in v5:
time: 65.7 us; the launch traced here: 65.4 us
  Pallas kernels  61.7 us (94%)
  local copies, waits for them, and re-layouts  3.11 us (5%)
    pallas_call x1, Pallas kernels, body(): pl.pallas_call(functools.partial(kernel, n_lat, n_lon), out_shape=shapes,...  61.7 us
    unnamed x7, local copies, waits for them, and re-layouts  3.11 us

profile of v5, /device:TPU:1, one launch (start us, length us, event | category | flops | bytes accessed | tf_op | source)
XLA Modules:
  0.0 65.4 jit_solution(16910674683557922602)
XLA Ops:
  0.6 61.7 %shard_map.121 = (f32[16,16,256]{2,1,0:T(8,128)}, f32[8,1024]{1,0:T(8,128)}, f32[8,1536]{1,0:T(8,128)}) custom-call(bf16[16,16,180]{2,1,0:T(8,128)(2,1)} %feat_in.1, bf16[16,16,180]{2,1,0:T(8,128)(2,1)} %cot_in_hbm.1, f32[1,180]{1,0:T(1,128)} %bitcast.8, bf16[180,540]{1,0:T(8,128)(2,1)} %qkv1_in.1, bf16[180,180]{1,0:T(8,128)(2,1)} %proj1_in.1, ...), custom_call_target="tpu_custom_call" | custom-call | tf_op jit(solution)/shard_map/pallas_call | solution.py:920
  62.3 0.0 copy-start.1
  62.3 1.7 %copy.16 = f32[16,16,180]{2,1,0:T(8,128)} copy(f32[16,16,180]{2,1,0:T(8,128)} %bitcast.5) | data formatting | bytes 368640
  64.0 0.0 copy-done.1
  64.0 0.0 copy-start
  64.0 0.6 copy.17
  64.6 0.2 copy-done
  64.8 0.6 copy.18
Async XLA Ops:
  62.3 1.7 %copy-start.1 = (f32[8,1024]{1,0:T(8,128)S(1)}, f32[8,1024]{1,0:T(8,128)}, u32[]{:S(2)}) copy-start(f32[8,1024]{1,0:T(8,128)} %get-tuple-element.7) | copy-start | bytes 98308
  64.0 0.8 %copy-start = (f32[8,1536]{1,0:T(8,128)S(1)}, f32[8,1536]{1,0:T(8,128)}, u32[]{:S(2)}) copy-start(f32[8,1536]{1,0:T(8,128)} %get-tuple-element.8) | copy-start | bytes 147460

commit v6 on v5

--- a/solution.py
+++ b/solution.py
@@ -302,7 +302,7 @@
         for s in range(3):
             start = dy * CROSS + 8 * s
             flat2[s, :, dy * 32 : dy * 32 + 23] = tab2_ref[:, start : start + 23]
-    def spread(group, _):
+    def spread(group):
         for i in range(3):
             h = 3 * group + i
             row = pl.ds(h, 1)
@@ -314,9 +314,9 @@
                 base = jnp.broadcast_to(flat2[s, row, :] * LOG2E, (8, LANES_C))
                 for r, part in enumerate(spread_rows(base, -1, 4)):
                     z2[s, r, h] = part[:, :USED_C]
-        return 0
-
-    lax.fori_loop(0, HEADS // 3, spread, 0)
+
+    for group in range(HEADS // 3):
+        spread(group)
     query_half = (iota((1, CELLS), 1) >> 4) & 1
 
     def window_bias(h, y8):
@@ -404,6 +404,14 @@
             rows = slice(h * CELLS, (h + 1) * CELLS)
             into[rows, half : half + 128] = own_lanes
             into[rows, 128 - half : 256 - half] = zeros
+
+    cot = cot_ref[...].astype(F32)
+    cot_own = [
+        cot[8 * sy : 8 * sy + 8, 8 * sx : 8 * sx + 8, :].reshape(64, CHANNELS)
+        for sy, sx, w, s in OWN
+    ]
+    cot_in = dot(turn[0], jnp.concatenate(cot_own, axis=0).astype(BF16)).astype(BF16)
+    gt[...] = dot_nt(pp2[...], cot_in)
 
     every = region.at[pl.ds(0, 3)]
     pltpu.make_async_copy(every, every, halo_recv).wait()
@@ -498,14 +506,7 @@
         axis=0,
     )
     queries_in = dot(turn[0], own_second.astype(BF16)).astype(BF16)
-    cot = cot_ref[...].astype(F32)
-    cot_own = [
-        cot[8 * sy : 8 * sy + 8, 8 * sx : 8 * sx + 8, :].reshape(64, CHANNELS)
-        for sy, sx, w, s in OWN
-    ]
-    cot_in = dot(turn[0], jnp.concatenate(cot_own, axis=0).astype(BF16)).astype(BF16)
     queries_t = dot_nt(wt2[0:WIDE, :], queries_in).astype(BF16)
-    gt[...] = dot_nt(pp2[...], cot_in)
     for h in range(HEADS):
         qmt[0, h] = head_rows(queries_t[h * HEAD_PAD : (h + 1) * HEAD_PAD, :], h)
     head_lanes(dot_nt(queries_in, wt2[0:WIDE, :]), qm)
@@ -680,15 +681,15 @@
         for s in range(3):
             collect(acc2, h, s, KEY_SIDE, lambda m: (m * 3 + s) * 8, s2.at[h])
 
-    def gather_cross(group, _):
+    def gather_cross(group):
         for i in range(3):
             h = 3 * group + i
             for s in range(3):
                 parts = [widened(acc2[s, r, h], LANES_C) for r in range(4)]
                 flat2[s, pl.ds(h, 1), :] = gather_rows(parts, -1)
-        return 0
-
-    lax.fori_loop(0, HEADS // 3, gather_cross, 0)
+
+    for group in range(HEADS // 3):
+        gather_cross(group)
     dense2[...] = jnp.zeros(dense2.shape, F32)
     for dy in range(CROSS):
         for s in range(3):

time: 65.7 us -> 66.7 us (1.015)
  Pallas kernels: 61.7 us -> 62.7 us
    pallas_call x1, Pallas kernels: 61.7 us -> 62.7 us  [body(): pl.pallas_call(functools.partial(kernel, n_lat, n_lon), out_shape=shapes,...]
where the time goes in v6:
time: 66.7 us; the launch traced here: 66.5 us
  Pallas kernels  62.7 us (94%)
  local copies, waits for them, and re-layouts  3.11 us (5%)
    pallas_call x1, Pallas kernels, body(): pl.pallas_call(functools.partial(kernel, n_lat, n_lon), out_shape=shapes,...  62.7 us
    unnamed x7, local copies, waits for them, and re-layouts  3.11 us

profile of v6, /device:TPU:1, one launch (start us, length us, event | category | flops | bytes accessed | tf_op | source)
XLA Modules:
  0.0 66.5 jit_solution(2819706170718880132)
XLA Ops:
  0.6 62.7 %shard_map.121 = (f32[16,16,256]{2,1,0:T(8,128)}, f32[8,1024]{1,0:T(8,128)}, f32[8,1536]{1,0:T(8,128)}) custom-call(bf16[16,16,180]{2,1,0:T(8,128)(2,1)} %feat_in.1, bf16[16,16,180]{2,1,0:T(8,128)(2,1)} %cot_in_hbm.1, f32[1,180]{1,0:T(1,128)} %bitcast.8, bf16[180,540]{1,0:T(8,128)(2,1)} %qkv1_in.1, bf16[180,180]{1,0:T(8,128)(2,1)} %proj1_in.1, ...), custom_call_target="tpu_custom_call" | custom-call | tf_op jit(solution)/shard_map/pallas_call | solution.py:921
  63.4 0.0 copy-start.1
  63.4 1.7 %copy.16 = f32[16,16,180]{2,1,0:T(8,128)} copy(f32[16,16,180]{2,1,0:T(8,128)} %bitcast.5) | data formatting | bytes 368640
  65.0 0.0 copy-done.1
  65.0 0.0 copy-start
  65.0 0.6 copy.17
  65.7 0.2 copy-done
  65.9 0.6 copy.18
Async XLA Ops:
  63.4 1.7 %copy-start.1 = (f32[8,1024]{1,0:T(8,128)S(1)}, f32[8,1024]{1,0:T(8,128)}, u32[]{:S(2)}) copy-start(f32[8,1024]{1,0:T(8,128)} %get-tuple-element.7) | copy-start | bytes 98308
  65.0 0.8 %copy-start = (f32[8,1536]{1,0:T(8,128)S(1)}, f32[8,1536]{1,0:T(8,128)}, u32[]{:S(2)}) copy-start(f32[8,1536]{1,0:T(8,128)} %get-tuple-element.8) | copy-start | bytes 147460
